TPU v7x, 128 devices: a whole 4x4x4 slice. The times are simulated.
128 devices in a mesh: gx: 8 (over z, core), gy: 16 (over y, x).
Axes of the slice: x: 4, y: 4, z: 4, core: 2. Of those that a mesh axis runs over, the one named last changes fastest.
Arguments:
- seed_grad: float32 [3, 64, 128, 128], P(None, 'gx', 'gy'), may hold values from -8 to 8
- modulus: float32 [64, 128, 128], P('gx', 'gy'), may hold values from 0.5 to 4
- lumped_mass: float32 [64, 128, 128], P('gx', 'gy'), may hold values from 0.3 to 3
- pair_dest: int32 [131072, 1], P(('gx', 'gy')), may hold values from 0 to 15; in each aligned block of 1024 rows (0 to 1023, 1024 to 2047, ...) at most 256 rows name the same one
- slave_nodes: int32 [4, 131072], P(None, ('gx', 'gy')), may hold values from 0 to 8191
- slave_weights: float32 [4, 131072], P(None, ('gx', 'gy')), may hold values from 0.2 to 1
- master_nodes: int32 [4, 131072], P(None, ('gx', 'gy')), may hold values from 0 to 8191
- master_weights: float32 [4, 131072], P(None, ('gx', 'gy')), may hold values from 0.2 to 1
- penalty: float32 [131072], P(('gx', 'gy')), may hold values from 0.5 to 4
Outputs:
- adjoint: float32 [3, 64, 128, 128], P(None, 'gx', 'gy')
- residual: float32 [3, 64, 128, 128], P(None, 'gx', 'gy')
Inputs may be any that keep to these rules, and one draw needn't show every extreme that they name: `pair_dest`: in the rows of one device at most 256 segments name the same gy index, a bound that some block reaches of them.
All inputs are finite; a program needn't handle non-finite values.
Results may differ from a plain program's by a relative error of at most 0.00021.
Values sent between devices are 32-bit elements; how exact they have to be, the bound alone decides.
A program may use at most 192 MiB of HBM per device.

v0:
```python
import math

import jax
import jax.numpy as jnp
import numpy as np
from jax import lax
from jax.sharding import PartitionSpec as P

ITERS = 2
CAP = 256


shear_ratio = 1.0 / 2.6
lame_ratio = 0.3 / 0.52


def with_halo(block, sides, width):
    for axis, dim in sides:
        count = lax.axis_size(axis)
        forward = [(i, i + 1) for i in range(count - 1)]
        backward = [(target, source) for source, target in forward]
        low = lax.ppermute(
            lax.slice_in_dim(block, block.shape[dim] - width, None, axis=dim), axis, forward
        )
        high = lax.ppermute(lax.slice_in_dim(block, 0, width, axis=dim), axis, backward)
        block = jnp.concatenate([low, block, high], axis=dim)
    return block


def shape_tables():
    abscissa = 1.0 / math.sqrt(3.0)
    points = [
        (a, b, c)
        for a in (-abscissa, abscissa)
        for b in (-abscissa, abscissa)
        for c in (-abscissa, abscissa)
    ]
    offsets = [
        (i, j, k)
        for i in range(3)
        for j in range(3)
        for k in range(3)
        if (i == 1) + (j == 1) + (k == 1) <= 1
    ]
    corners = [(i, j, k) for i in (0, 2) for j in (0, 2) for k in (0, 2)]
    derivative = np.zeros((8, 3, 20))
    trilinear = np.zeros((8, 8))
    for g, location in enumerate(points):
        for n, offset in enumerate(offsets):
            natural = [offset[d] - 1 for d in range(3)]
            factors = [
                1.0 - location[d] ** 2 if natural[d] == 0 else 1.0 + location[d] * natural[d]
                for d in range(3)
            ]
            slopes = [
                -2.0 * location[d] if natural[d] == 0 else float(natural[d]) for d in range(3)
            ]
            linear = (
                location[0] * natural[0] + location[1] * natural[1] + location[2] * natural[2] - 2.0
            )
            for d in range(3):
                others = factors[(d + 1) % 3] * factors[(d + 2) % 3]
                if 0 in natural:
                    derivative[g, d, n] = slopes[d] * others / 4.0
                else:
                    derivative[g, d, n] = natural[d] * others * (linear + factors[d]) / 8.0
        for c, corner in enumerate(corners):
            weight = 1.0
            for d in range(3):
                weight = weight * (1.0 + location[d] * (corner[d] - 1)) / 2.0
            trilinear[g, c] = weight
    return (derivative, trilinear, offsets, corners)


def strided(first, count):
    return slice(first, first + 2 * count - 1, 2)


def gather_nodes(padded, counts, offsets):
    return jnp.stack(
        [
            padded[:, strided(o[0], counts[0]), strided(o[1], counts[1]), strided(o[2], counts[2])]
            for o in offsets
        ]
    )


def spread_nodes(values, target_shape, counts, offsets):
    result = jnp.zeros(target_shape, jnp.float32)
    for n, offset in enumerate(offsets):
        result = result.at[
            :,
            strided(offset[0], counts[0]),
            strided(offset[1], counts[1]),
            strided(offset[2], counts[2]),
        ].add(values[n])
    return result


def gauss_moduli(padded_mod, counts, corners, trilinear):
    corner_values = jnp.stack(
        [
            padded_mod[strided(c[0], counts[0]), strided(c[1], counts[1]), strided(c[2], counts[2])]
            for c in corners
        ]
    ).reshape(8, -1)
    moduli = jnp.einsum(
        "gc,ce->ge",
        jnp.asarray(trilinear, jnp.float32),
        corner_values,
        precision=lax.Precision.HIGHEST,
    )
    return (moduli * shear_ratio, moduli * lame_ratio)


def element_forces(padded, padded_mod, counts):
    derivative, trilinear, offsets, corners = shape_tables()
    slope_table = jnp.asarray(derivative, jnp.float32)
    shear_modulus, lame_lambda_modulus = gauss_moduli(padded_mod, counts, corners, trilinear)
    stacked = gather_nodes(padded, counts, offsets).reshape(20, -1)
    gradients = jnp.einsum(
        "gan,nm->gam", slope_table, stacked, precision=lax.Precision.HIGHEST
    ).reshape(8, 3, 3, -1)
    dilation = gradients[:, 0, 0] + gradients[:, 1, 1] + gradients[:, 2, 2]
    identity = jnp.eye(3, dtype=jnp.float32)[None, :, :, None]
    stress = (
        shear_modulus[:, None, None] * (gradients + jnp.swapaxes(gradients, 1, 2))
        + (lame_lambda_modulus * dilation)[:, None, None] * identity
    )
    forces = jnp.einsum(
        "gan,gam->nm", slope_table, stress.reshape(8, 3, -1), precision=lax.Precision.HIGHEST
    )
    return spread_nodes(forces.reshape((20, 3) + tuple(counts)), padded.shape, counts, offsets)


def element_diagonal(padded_mod, counts, target_shape):
    derivative, trilinear, offsets, corners = shape_tables()
    slope_table = jnp.asarray(derivative, jnp.float32)
    shear_modulus, lame_lambda_modulus = gauss_moduli(padded_mod, counts, corners, trilinear)
    squared_terms = slope_table * slope_table
    summed_squares = jnp.sum(squared_terms, axis=1)
    first_part = jnp.einsum(
        "gn,ge->ne", summed_squares, shear_modulus, precision=lax.Precision.HIGHEST
    )
    second_share = jnp.einsum(
        "rtc,ry->cty",
        squared_terms,
        shear_modulus + lame_lambda_modulus,
        precision=lax.Precision.HIGHEST,
    )
    values = first_part[:, None, :] + second_share
    return spread_nodes(values.reshape((20, 3) + tuple(counts)), target_shape, counts, offsets)


def shards(
    seed_grad,
    modulus,
    lumped_mass,
    pair_dest,
    slave_nodes,
    slave_weights,
    master_nodes,
    master_weights,
    penalty,
):
    cells_x, cells_y, cells_z = modulus.shape
    counts = (cells_x // 2 + 1, cells_y // 2 + 1, cells_z // 2)
    padded_shape = (3, cells_x + 4, cells_y + 4, cells_z + 1)
    rim_modulus = jnp.pad(with_halo(modulus, (("gx", 0), ("gy", 1)), 2), ((0, 0), (0, 0), (0, 1)))

    def interior(full):
        return full[:, 2 : 2 + cells_x, 2 : 2 + cells_y, :cells_z]

    diagonal = interior(element_diagonal(rim_modulus, counts, padded_shape)) + lumped_mass
    inverse = 1.0 / diagonal
    group_size = lax.axis_size("gy")
    target = pair_dest[:, 0]
    onehot = (target[:, None] == jnp.arange(group_size, dtype=jnp.int32)[None, :]).astype(jnp.int32)
    position = jnp.sum((jnp.cumsum(onehot, axis=0) - 1) * onehot, axis=1)
    slot_index = target * CAP + position

    def place_slots(values):
        return (
            jnp.zeros((values.shape[0], group_size * CAP), jnp.float32)
            .at[:, slot_index]
            .set(values)
        )

    master_pack = place_slots(
        jnp.concatenate(
            [master_weights, penalty[None, :], master_nodes.astype(jnp.float32)], axis=0
        )
    )
    adjoint = jnp.zeros_like(seed_grad)
    residual = seed_grad

    def global_dot(first_vec, second_vec):
        return lax.psum(jnp.sum(first_vec * second_vec), ("gx", "gy"))

    precond = residual * inverse
    direction = precond
    precond_dot = global_dot(residual, precond)
    for iteration in range(ITERS):
        rimmed = jnp.pad(
            with_halo(direction, (("gx", 1), ("gy", 2)), 2), ((0, 0), (0, 0), (0, 0), (0, 1))
        )
        elastic = interior(element_forces(rimmed, rim_modulus, counts))
        flattened = direction.reshape(3, -1)
        slave_part = jnp.sum(flattened[:, slave_nodes] * slave_weights[None], axis=1)
        arrived = lax.all_to_all(
            jnp.concatenate([place_slots(slave_part), master_pack], axis=0),
            "gy",
            split_axis=1,
            concat_axis=1,
            tiled=True,
        )
        nearby_share = arrived[:3]
        remote_bundle = arrived[3:]
        far_weights = remote_bundle[:4]
        penalty_factors = remote_bundle[4]
        far_nodes = remote_bundle[5:9].astype(jnp.int32)
        master_surface_share = jnp.sum(flattened[:, far_nodes] * far_weights[None], axis=1)
        contact_traction = penalty_factors[None, :] * (nearby_share - master_surface_share)
        replied = lax.all_to_all(contact_traction, "gy", split_axis=1, concat_axis=1, tiled=True)
        returned = replied[:, slot_index]
        result = jnp.zeros_like(flattened)
        result = result.at[:, slave_nodes].add(slave_weights[None] * returned[:, None, :])
        result = result.at[:, far_nodes].add(-far_weights[None] * contact_traction[:, None, :])
        applied = elastic + lumped_mass * direction + result.reshape(direction.shape)
        step_size = precond_dot / global_dot(direction, applied)
        adjoint = adjoint + step_size * direction
        residual = residual - step_size * applied
        if iteration + 1 < ITERS:
            precond = residual * inverse
            new_dot = global_dot(residual, precond)
            direction = precond + new_dot / precond_dot * direction
            precond_dot = new_dot
    return (adjoint, residual)


def solution(mesh):
    placed = (
        P(None, "gx", "gy", None),
        P("gx", "gy", None),
        P("gx", "gy", None),
        P(("gx", "gy"), None),
        P(None, ("gx", "gy")),
        P(None, ("gx", "gy")),
        P(None, ("gx", "gy")),
        P(None, ("gx", "gy")),
        P(("gx", "gy")),
    )
    return jax.shard_map(
        shards,
        mesh=mesh,
        in_specs=placed,
        out_specs=(P(None, "gx", "gy", None), P(None, "gx", "gy", None)),
        check_vma=False,
    )
```

profile of v0, /device:TPU:1, one launch (start us, length us, event | category | flops | bytes accessed | tf_op | source)
XLA Modules:
  0.0 2070.5 jit_solution(4593888459047394722)
XLA Ops:
  140.7 18.3 scatter_fusion.5
  159.0 18.1 scatter_fusion.6
  213.2 18.5 scatter_fusion.9
  231.7 18.1 scatter_fusion.10
  285.9 18.3 scatter_fusion.13
  304.2 18.1 scatter_fusion.14
  358.4 18.3 scatter_fusion.17
  376.7 18.1 scatter_fusion.18
  612.2 18.1 scatter_fusion.23
  666.4 18.5 scatter_fusion.26
  684.9 18.1 scatter_fusion.27
  739.1 18.2 scatter_fusion.30
  757.4 18.1 scatter_fusion.31
  811.6 18.3 scatter_fusion.34
  829.9 18.1 scatter_fusion.35
  884.1 18.5 scatter_fusion.38
  902.6 18.1 scatter_fusion.39
  928.6 56.6 %gather_fusion.1 = f32[16384,3]{1,0:T(8,128)} fusion(f32[3,8192]{0,1:T(8,128)} %bitcast.277, s32[16384]{0:T(1024)S(1)} %broadcast_clamp_fusion.1), kind=kCustom, calls=%fused_computation.1 | custom fusion | bytes 458752 | tf_op jit(solution)/shard_map/gather | solution.py:222
  1016.9 24.7 %scatter_custom_fusion.2 = f32[3,8192]{0,1:T(8,128)} fusion(s32[4096]{0:T(1024)} %bitcast.437, f32[4096,3]{1,0:T(8,128)S(1)} %bitcast.287, f32[]{:T(128)} %constant.14.clone.1), kind=kCustom, calls=%fused_computation.95 | custom fusion | flops 12288 | bytes 98816 | tf_op jit(solution)/shard_map/scatter-add | solution.py:227
  1041.5 111.7 %scatter_fusion = f32[3,8192]{0,1:T(8,128)} fusion(f32[3,8192]{0,1:T(8,128)} %scatter_custom_fusion.2, s32[16384]{0:T(1024)S(1)} %bitcast.359, f32[16384,3]{1,0:T(8,128)} %bitcast.279), kind=kCustom, calls=%fused_computation.9 | custom fusion | flops 49152 | bytes 655360 | tf_op jit(solution)/shard_map/scatter-add | solution.py:228
  1157.6 69.2 %all-reduce.3 = (f32[]{:T(128)}, f32[]{:T(128)}) all-reduce(f32[]{:T(128)} %get-tuple-element.60, f32[]{:T(128)} %get-tuple-element.59), channel_id=1, replica_groups=mesh['gx'=8,'gy'=16] {'gx','gy'}, use_global_device_ids=true, to_apply=%region_22.23 | all-reduce | flops 2 | bytes 16 | tf_op jit(solution)/shard_map/psum | solution.py:198
  1229.8 62.9 %psum.30 = f32[]{:T(128)} all-reduce(f32[]{:T(128)} %get-tuple-element.107), channel_id=1, replica_groups=mesh['gx'=8,'gy'=16] {'gx','gy'}, use_global_device_ids=true, to_apply=%region_55.56 | all-reduce | flops 1 | bytes 8 | tf_op jit(solution)/shard_map/psum | solution.py:198
  1514.5 18.3 scatter_fusion.45
  1532.8 18.1 scatter_fusion.46
  1587.1 18.5 scatter_fusion.49
  1605.6 18.1 scatter_fusion.50
  1659.8 18.2 scatter_fusion.53
  1732.3 18.3 scatter_fusion.57
  1775.2 56.6 %gather_fusion.4 = f32[16384,3]{1,0:T(8,128)} fusion(f32[3,8192]{0,1:T(8,128)} %bitcast.275, s32[16384]{0:T(1024)S(1)} %broadcast_clamp_fusion), kind=kCustom, calls=%fused_computation.4 | custom fusion | bytes 458752 | tf_op jit(solution)/shard_map/gather | solution.py:222
  1860.5 24.7 %scatter_custom_fusion.5 = f32[3,8192]{0,1:T(8,128)} fusion(s32[4096]{0:T(1024)} %bitcast.438, f32[4096,3]{1,0:T(8,128)S(1)} %bitcast.286, f32[]{:T(128)} %constant.14.clone.1), kind=kCustom, calls=%fused_computation.93 | custom fusion | flops 12288 | bytes 98816 | tf_op jit(solution)/shard_map/scatter-add | solution.py:227
  1885.2 111.5 %scatter_fusion.1 = f32[3,8192]{0,1:T(8,128)} fusion(f32[3,8192]{0,1:T(8,128)} %scatter_custom_fusion.5, s32[16384]{0:T(1024)S(1)} %bitcast.357, f32[16384,3]{1,0:T(8,128)} %bitcast.278), kind=kCustom, calls=%fused_computation.12 | custom fusion | flops 49152 | bytes 655360 | tf_op jit(solution)/shard_map/scatter-add | solution.py:228
  2000.2 68.2 %psum.31 = f32[]{:T(128)} all-reduce(f32[]{:T(128)} %multiply_reduce_fusion.4), channel_id=1, replica_groups=mesh['gx'=8,'gy'=16] {'gx','gy'}, use_global_device_ids=true, to_apply=%region_82.83 | all-reduce | flops 1 | bytes 8 | tf_op jit(solution)/shard_map/psum | solution.py:198
  (645 shorter events, 1058.5 us)
Async XLA Ops:
  1.5 23.1 %collective-permute-start = (f32[2,8,128]{2,1,0:T(8,128)S(1)}, f32[2,8,128]{2,1,0:T(8,128)S(1)}, u32[]{:S(2)}, u32[]{:S(2)}) collective-permute-start(f32[2,8,128]{2,1,0:T(8,128)S(1)} %get-tuple-element.153), channel_id=1, source_target_pairs={{0,16},{16,32},{32,48},{48,64},{64,80},{80,96},{96,112},{1,17},{17... | collective-permute-start | bytes 24584 | tf_op jit(solution)/shard_map/ppermute | solution.py:22
  6.4 18.9 collective-permute-start.1
  25.4 12.6 collective-permute-start.2
  28.5 9.5 collective-permute-start.3
  32.1 634.3 %copy-start.24 = (s32[1600]{0:T(1024)}, s32[1600]{0:T(1024)S(1)}, u32[]{:S(2)}) copy-start(s32[1600]{0:T(1024)S(1)} %reshape.830) | copy-start | bytes 19204
  32.2 652.7 %copy-start.22 = (s32[1600]{0:T(1024)}, s32[1600]{0:T(1024)S(1)}, u32[]{:S(2)}) copy-start(s32[1600]{0:T(1024)S(1)} %reshape.836) | copy-start | bytes 19204
  32.3 670.7 %copy-start.20 = (s32[1600]{0:T(1024)}, s32[1600]{0:T(1024)S(1)}, u32[]{:S(2)}) copy-start(s32[1600]{0:T(1024)S(1)} %reshape.842) | copy-start | bytes 19204
  32.3 688.7 %copy-start.18 = (s32[1600]{0:T(1024)}, s32[1600]{0:T(1024)S(1)}, u32[]{:S(2)}) copy-start(s32[1600]{0:T(1024)S(1)} %reshape.848) | copy-start | bytes 19204
  32.4 706.7 %copy-start.16 = (s32[1600]{0:T(1024)}, s32[1600]{0:T(1024)S(1)}, u32[]{:S(2)}) copy-start(s32[1600]{0:T(1024)S(1)} %reshape.854) | copy-start | bytes 19204
  32.5 724.9 %copy-start.14 = (s32[1600]{0:T(1024)}, s32[1600]{0:T(1024)S(1)}, u32[]{:S(2)}) copy-start(s32[1600]{0:T(1024)S(1)} %reshape.860) | copy-start | bytes 19204
  32.6 742.9 %copy-start.12 = (s32[1600]{0:T(1024)}, s32[1600]{0:T(1024)S(1)}, u32[]{:S(2)}) copy-start(s32[1600]{0:T(1024)S(1)} %reshape.866) | copy-start | bytes 19204
  32.6 760.9 %copy-start.10 = (s32[1600]{0:T(1024)}, s32[1600]{0:T(1024)S(1)}, u32[]{:S(2)}) copy-start(s32[1600]{0:T(1024)S(1)} %reshape.872) | copy-start | bytes 19204
  32.7 778.9 %copy-start.8 = (s32[1600]{0:T(1024)}, s32[1600]{0:T(1024)S(1)}, u32[]{:S(2)}) copy-start(s32[1600]{0:T(1024)S(1)} %reshape.878) | copy-start | bytes 19204
  32.8 797.1 %copy-start.6 = (s32[1600]{0:T(1024)}, s32[1600]{0:T(1024)S(1)}, u32[]{:S(2)}) copy-start(s32[1600]{0:T(1024)S(1)} %reshape.884) | copy-start | bytes 19204
  32.9 815.1 %copy-start.4 = (s32[1600]{0:T(1024)}, s32[1600]{0:T(1024)S(1)}, u32[]{:S(2)}) copy-start(s32[1600]{0:T(1024)S(1)} %reshape.890) | copy-start | bytes 19204
  32.9 833.1 %copy-start.2 = (s32[1600]{0:T(1024)}, s32[1600]{0:T(1024)S(1)}, u32[]{:S(2)}) copy-start(s32[1600]{0:T(1024)S(1)} %reshape.896) | copy-start | bytes 19204
  44.2 427.3 %copy-start.49 = (f32[1600]{0:T(1024)}, f32[1600]{0:T(1024)S(1)}, u32[]{:S(2)}) copy-start(f32[1600]{0:T(1024)S(1)} %reshape.609) | copy-start | bytes 19204
  44.3 427.2 %copy-start.52 = (f32[1600]{0:T(1024)}, f32[1600]{0:T(1024)S(1)}, u32[]{:S(2)}) copy-start(f32[1600]{0:T(1024)S(1)} %reshape.611) | copy-start | bytes 19204
  44.3 427.1 %copy-start.54 = (f32[1600]{0:T(1024)}, f32[1600]{0:T(1024)S(1)}, u32[]{:S(2)}) copy-start(f32[1600]{0:T(1024)S(1)} %reshape.613) | copy-start | bytes 19204
  440.4 25.0 %collective-permute-start.4 = (f32[3,2,8,128]{3,2,1,0:T(8,128)S(1)}, f32[3,2,8,128]{3,2,1,0:T(8,128)S(1)}, u32[]{:S(2)}, u32[]{:S(2)}) collective-permute-start(f32[3,2,8,128]{3,2,1,0:T(8,128)S(1)} %get-tuple-element.128), channel_id=1, source_target_pairs={{0,16},{16,32},{32,48},{48,64},{64,80},{80,96},{96,112},{1,17},{17... | collective-permute-start | bytes 73736 | tf_op jit(solution)/shard_map/ppermute | solution.py:22
  444.3 21.1 %collective-permute-start.5 = (f32[3,2,8,128]{3,2,1,0:T(8,128)S(1)}, f32[3,2,8,128]{3,2,1,0:T(8,128)S(1)}, u32[]{:S(2)}, u32[]{:S(2)}) collective-permute-start(f32[3,2,8,128]{3,2,1,0:T(8,128)S(1)} %get-tuple-element.129), channel_id=1, source_target_pairs={{16,0},{32,16},{48,32},{64,48},{80,64},{96,80},{112,96},{17,1},{33... | collective-permute-start | bytes 73736 | tf_op jit(solution)/shard_map/ppermute | solution.py:25
  465.5 16.6 collective-permute-start.6
  469.7 12.4 collective-permute-start.7
  472.7 455.2 %all-to-all-start = ((f32[12,16,256]{2,0,1:T(8,128)}), f32[12,16,256]{2,0,1:T(8,128)S(1)}, u32[]{:S(2)}, u32[]{:S(2)}) async-start(f32[12,16,256]{2,0,1:T(8,128)} %copy.397), calls=%async_computation | async-start | bytes 524288 | tf_op jit(solution)/shard_map/all_to_all | solution.py:210
  996.9 13.7 all-to-all-start.1
  1296.8 23.4 %collective-permute-start.8 = (f32[3,2,8,128]{3,2,1,0:T(8,128)S(1)}, f32[3,2,8,128]{3,2,1,0:T(8,128)S(1)}, u32[]{:S(2)}, u32[]{:S(2)}) collective-permute-start(f32[3,2,8,128]{3,2,1,0:T(8,128)S(1)} %get-tuple-element.126), channel_id=1, source_target_pairs={{0,16},{16,32},{32,48},{48,64},{64,80},{80,96},{96,112},{1,17},{17... | collective-permute-start | bytes 73736 | tf_op jit(solution)/shard_map/ppermute | solution.py:22
  1300.2 20.0 collective-permute-start.9
  1320.2 11.1 collective-permute-start.10
  1321.8 9.6 collective-permute-start.11
  1324.1 450.9 %all-to-all-start.2 = ((f32[12,16,256]{2,0,1:T(8,128)}), f32[12,16,256]{2,0,1:T(8,128)S(1)}, u32[]{:S(2)}, u32[]{:S(2)}) async-start(f32[12,16,256]{2,0,1:T(8,128)} %copy.431), calls=%async_computation.2 | async-start | bytes 524288 | tf_op jit(solution)/shard_map/all_to_all | solution.py:210
  1422.3 291.9 %copy-start.3 = (s32[1600]{0:T(1024)S(1)}, s32[1600]{0:T(1024)}, u32[]{:S(2)}) copy-start(s32[1600]{0:T(1024)} %copy-done.2) | copy-start | bytes 19204
  1840.5 13.7 all-to-all-start.3
  (79 other events, 5565.8 us)
where the time goes:
time: 2080 us; the launch traced here: 2070 us
  other arithmetic  1410 us (68%)
  local copies, waits for them, and re-layouts  385 us (19%)
  blocking collectives  200 us (10%)
  starting transfers between devices  61.3 us (3%)
    unnamed x77, other arithmetic  1090 us
    scatter-add x2, other arithmetic, shards(): result.at[:, far_nodes]  223 us
    psum x3, blocking collectives, global_dot(): return lax.psum(jnp.sum(first_vec * second_vec), ('gx', 'gy'))  200 us
    gather x2, local copies, waits for them, and re-layouts, shards(): flattened[:, far_nodes] * far_weights[None]  113 us
    slice x40, local copies, waits for them, and re-layouts, gather_nodes(): padded[:, strided(o[0], counts[0]), strided(o[1], counts[1]), strided(o[2...  88.9 us
    squeeze x120, local copies, waits for them, and re-layouts, spread_nodes(): values[n]  71.6 us
    scatter-add x2, other arithmetic, shards(): result.at[:, slave_nodes].add(slave_weights[None] * returned[:, None, :])  49.3 us
  transfers between devices with their start and end apart: 16, of which 0 were waited for; matrix products, arithmetic and copies ran while one was open for 47% of the time, Pallas kernels for 0%

commit v1 on v0

v1 whole, which is shorter than its diff:
```python
import functools
import math

import jax
import jax.numpy as jnp
import numpy as np
from jax import lax
from jax.experimental import pallas as pl
from jax.experimental.pallas import tpu as pltpu
from jax.sharding import PartitionSpec as P

CAP = 256
SHEAR = 1.0 / 2.6
LAME = 0.3 / 0.52
MESH = pl.DeviceIdType.MESH
F32 = jnp.float32
BF16 = jnp.bfloat16
VMEM = pl.BlockSpec(memory_space=pltpu.VMEM)
LIMIT = 40 * 1024 * 1024

WIDE = 72


def shape_tables():
    abscissa = 1.0 / math.sqrt(3.0)
    points = [
        (a, b, c)
        for a in (-abscissa, abscissa)
        for b in (-abscissa, abscissa)
        for c in (-abscissa, abscissa)
    ]
    offsets = [
        (i, j, k)
        for i in range(3)
        for j in range(3)
        for k in range(3)
        if (i == 1) + (j == 1) + (k == 1) <= 1
    ]
    derivative = np.zeros((8, 3, 20))
    for g, location in enumerate(points):
        for n, offset in enumerate(offsets):
            natural = [offset[d] - 1 for d in range(3)]
            factors = [
                1.0 - location[d] ** 2 if natural[d] == 0 else 1.0 + location[d] * natural[d]
                for d in range(3)
            ]
            slopes = [
                -2.0 * location[d] if natural[d] == 0 else float(natural[d]) for d in range(3)
            ]
            linear = sum(location[d] * natural[d] for d in range(3)) - 2.0
            for d in range(3):
                others = factors[(d + 1) % 3] * factors[(d + 2) % 3]
                if 0 in natural:
                    derivative[g, d, n] = slopes[d] * others / 4.0
                else:
                    derivative[g, d, n] = natural[d] * others * (linear + factors[d]) / 8.0
    return derivative, offsets


def signs(count, dims):
    table = np.ones((count, count))
    for t in range(count):
        for c in range(count):
            for d in range(dims):
                if t >> d & 1 and not c >> d & 1:
                    table[t, c] = -table[t, c]
    return table


def element_tables():
    derivative, offsets = shape_tables()
    eight, four = signs(8, 3), signs(4, 2)
    modal = np.einsum("sg,gan->asn", eight, derivative) / 8.0
    corner_at = [offsets.index((c >> 2 << 1, (c >> 1 & 1) << 1, (c & 1) << 1)) for c in range(8)]
    edge_at = []
    for d in range(3):
        row = []
        for c in range(4):
            offset = [(c >> 1) << 1, (c & 1) << 1]
            offset.insert(d, 1)
            row.append(offsets.index(tuple(offset)))
        edge_at.append(row)
    corner_terms = np.einsum("tn,asn->ast", eight, modal[:, :, corner_at]) / 8.0
    edge_terms = [np.einsum("tn,asn->ast", four, modal[:, :, edge_at[d]]) / 4.0 for d in range(3)]
    trilinear = np.array([(1.0 / math.sqrt(3.0)) ** bin(t).count("1") / 8.0 for t in range(8)])
    at_points = np.einsum("t,tg->gt", trilinear, eight)
    squares = derivative * derivative
    weight = np.einsum(
        "gt,gni->tni",
        at_points,
        SHEAR * squares.sum(axis=1)[:, :, None] + (LAME + SHEAR) * np.swapaxes(squares, 1, 2),
    )
    corner_diag = np.einsum("un,tni->uti", eight, weight[:, corner_at]) / 8.0
    edge_diag = [np.einsum("un,tni->uti", four, weight[:, edge_at[d]]) / 4.0 for d in range(3)]
    return corner_terms, edge_terms, trilinear, corner_diag, edge_diag


def split_sums(values):
    values = list(values)
    step = 1
    while step < len(values):
        for low in range(len(values)):
            if not low & step:
                a, b = values[low], values[low | step]
                values[low], values[low | step] = b + a, b - a
        step *= 2
    return values


def join_sums(values):
    values = list(values)
    step = 1
    while step < len(values):
        for low in range(len(values)):
            if not low & step:
                a, b = values[low], values[low | step]
                values[low], values[low | step] = a - b, a + b
        step *= 2
    return values


def combine(terms):
    total = None
    for factor, value in terms:
        if abs(factor) < 1e-12:
            continue
        term = value * np.float32(factor)
        total = term if total is None else total + term
    return total


def lanes(rows):
    return lax.broadcasted_iota(jnp.int32, (rows, 128), 1)


def shift_down(value):
    return jnp.where(lanes(value.shape[0]) == 63, 0.0, pltpu.roll(value, 127, 1))


def collect(low, middle, high):
    total = low + jnp.where(lanes(8) < 64, pltpu.roll(high, 1, 1), 0.0)
    if middle is not None:
        total = total + pltpu.roll(middle, 64, 1)
    return total


def corner_moduli(wide_mod, wide_mod_up, group):
    values = []
    for c in range(8):
        ref = wide_mod_up if c & 1 else wide_mod
        values.append(ref[pl.ds(8 * (group + (c >> 2)) + (c >> 1 & 1), 8), :])
    inside = lanes(8) < 64
    return split_sums([jnp.where(inside, value, 0.0) for value in values])


def edge_corner(d, c):
    where = [c >> 1, c & 1]
    where.insert(d, None)
    return where


def add_rows(ref, index, row, value):
    ref[index + (pl.ds(row, 8), slice(None))] += value


def scatter_forces(out, i, corner, edges, group):
    for xy in range(4):
        row = 8 * (group + (xy >> 1)) + (xy & 1)
        add_rows(out, (i, 0), row, collect(corner[2 * xy], edges[2][xy], corner[2 * xy + 1]))
    for y in range(2):
        add_rows(out, (i, 2), 8 * group + y, collect(edges[0][2 * y], None, edges[0][2 * y + 1]))
    for x in range(2):
        add_rows(
            out, (i, 1), 8 * (group + x), collect(edges[1][2 * x], None, edges[1][2 * x + 1])
        )


def diagonal_into(out, wide_mod, wide_mod_up):
    corner_diag, edge_diag = element_tables()[3:]
    out[...] = jnp.zeros_like(out)
    for group in range(7):
        moduli = corner_moduli(wide_mod, wide_mod_up, group)
        for i in range(3):
            corner = join_sums(
                [
                    combine([(corner_diag[u, t, i], moduli[t]) for t in range(8)])
                    for u in range(8)
                ]
            )
            edges = [
                join_sums(
                    [
                        combine([(edge_diag[d][u, t, i], moduli[t]) for t in range(8)])
                        for u in range(4)
                    ]
                )
                for d in range(3)
            ]
            scatter_forces(out, i, corner, edges, group)


def stiffness_into(out, wide, wide_up, wide_mid, wide_mod, wide_mod_up):
    corner_terms, edge_terms, trilinear = element_tables()[:3]
    out[...] = jnp.zeros_like(out)
    for group in range(1, 6):
        moduli = corner_moduli(wide_mod, wide_mod_up, group)
        points = join_sums([moduli[t] * np.float32(trilinear[t]) for t in range(8)])
        slopes = []
        for i in range(3):
            corner = []
            for c in range(8):
                ref = wide_up if c & 1 else wide
                corner.append(ref[i, 0, pl.ds(8 * (group + (c >> 2)) + (c >> 1 & 1), 8), :])
            corner = split_sums(corner)
            edges = []
            for d in range(3):
                values = []
                for c in range(4):
                    x, y, z = edge_corner(d, c)
                    row = 8 * (group + (x or 0)) + (y or 0)
                    parity = (2, 1, 0)[d]
                    if d == 2:
                        values.append(wide_mid[i, pl.ds(row, 8), :])
                    else:
                        values.append((wide_up if z else wide)[i, parity, pl.ds(row, 8), :])
                edges.append(split_sums(values))
            slopes.append(
                [
                    [
                        combine(
                            [(corner_terms[a, s, t], corner[t]) for t in range(8)]
                            + [
                                (edge_terms[d][a, s, t], edges[d][t])
                                for d in range(3)
                                for t in range(4)
                            ]
                        )
                        for s in range(8)
                    ]
                    for a in range(3)
                ]
            )

        def plus(a, b):
            return a if b is None else b if a is None else a + b

        zero = jnp.zeros((8, 128), F32)
        strain = {}
        for a in range(3):
            strain[a, a] = slopes[a][a]
            for b in range(a):
                strain[b, a] = [plus(p, q) for p, q in zip(slopes[a][b], slopes[b][a])]
        strain = {
            key: join_sums([zero if v is None else v for v in value])
            for key, value in strain.items()
        }
        stress = {key: [] for key in strain}
        for g in range(8):
            volume = (strain[0, 0][g] + strain[1, 1][g] + strain[2, 2][g]) * np.float32(LAME)
            for a in range(3):
                stress[a, a].append(
                    points[g] * (volume + strain[a, a][g] * np.float32(2.0 * SHEAR))
                )
            scaled = points[g] * np.float32(SHEAR)
            for key in ((0, 1), (0, 2), (1, 2)):
                stress[key].append(scaled * strain[key][g])
        stress = {key: split_sums(value) for key, value in stress.items()}
        for i in range(3):
            pairs = [
                (a, s, stress[min(a, i), max(a, i)][s]) for a in range(3) for s in range(8)
            ]
            corner = join_sums(
                [combine([(corner_terms[a, s, t], v) for a, s, v in pairs]) for t in range(8)]
            )
            edges = [
                join_sums(
                    [combine([(edge_terms[d][a, s, t], v) for a, s, v in pairs]) for t in range(4)]
                )
                for d in range(3)
            ]
            scatter_forces(out, i, corner, edges, group)


def lift(wide, wide_up, wide_mid):
    for i in range(3):
        for parity in range(3):
            wide_up[i, parity] = shift_down(wide[i, parity])
        wide_mid[i] = pltpu.roll(wide[i, 0], 64, 1)


def halo_plan(fields, with_modulus):
    plan, first = [], 0
    for dx in (-1, 0, 1):
        for dy in (-1, 0, 1):
            if dx == 0 and dy == 0:
                continue
            pieces = []

            def places(step, both):
                if step == 1:
                    return [(p, 3, 1) for p in ((0, 1) if both else (0,))]
                return [(0, 0, 6)]

            def strips(array, xs, ys):
                for px, ox, wx in xs:
                    for py, oy, wy in ys:
                        if ox is None:
                            pieces.append((array, px * 2 + py, oy, 4, 4, 8 * 2 + wy, 8))
                        elif oy is None:
                            pieces.append((array, px * 2 + py, 4 * ox, 4, 1, 8 * wx + 2, 1))
                        else:
                            pieces.append((array, px * 2 + py, 4 * ox + oy, 1, 1, 8 * wx + wy, 1))

            every = [(0, None, None), (1, None, None)]
            for array in range(fields):
                strips(
                    array,
                    every if dx == 0 else places(dx, True),
                    every if dy == 0 else places(dy, True),
                )
            if with_modulus:
                deep = {1: [(0, 3, 1), (0, 2, 0)], -1: [(0, 0, 6), (0, 1, 7)], 0: every[:1]}
                strips(fields, deep[dx], deep[dy])
            rows = sum(piece[3] for piece in pieces)
            plan.append((dx, dy, first, -(-rows // 8) * 8, pieces))
            first += plan[-1][3]
    return plan, first


FIRST_PLAN, FIRST_ROWS = halo_plan(4, True)
NEXT_PLAN, NEXT_ROWS = halo_plan(3, False)


def rows_of(start, count, stride):
    return pl.ds(start, count) if stride == 1 else pl.ds(start, count, stride=stride)


def pack_halo(plan, own, message):
    message[...] = jnp.zeros_like(message)
    for _, _, first, _, pieces in plan:
        at = first
        for array, parity, start, count, stride, _, _ in pieces:
            source = own[rows_of(array * 64 + parity * 16 + start, count, stride), :]
            message[pl.ds(at, count), :] = source
            at += count


def unpack_halo(plan, extents, message, store):
    gx, gy = lax.axis_index("gx"), lax.axis_index("gy")
    for dx, dy, first, _, pieces in plan:
        inside = None
        for step, at, extent in ((dx, gx, extents[0]), (dy, gy, extents[1])):
            if step:
                here = at > 0 if step == 1 else at < extent - 1
                inside = here if inside is None else jnp.logical_and(inside, here)
        keep = jnp.where(inside, 1.0, 0.0).astype(F32)
        at = first
        for array, parity, _, count, _, start, stride in pieces:
            store(array, parity, start, count, stride, message[pl.ds(at, count), :] * keep)
            at += count


def widen_own(own, array, wide, i):
    for parity in range(4):
        for x in range(4):
            wide[i, parity, pl.ds(8 * (x + 2) + 2, 4), :] = own[
                pl.ds(array * 64 + parity * 16 + 4 * x, 4), :
            ]


def narrow(wide, i, own, array):
    for parity in range(4):
        for x in range(4):
            own[pl.ds(array * 64 + parity * 16 + 4 * x, 4), :] = wide[
                i, parity, pl.ds(8 * (x + 2) + 2, 4), :
            ]


def in_two(value):
    head = value.astype(BF16)
    return head, (value - head.astype(F32)).astype(BF16)


def down_iota(rows, columns):
    return lax.broadcasted_iota(jnp.int32, (rows, columns), 0).astype(F32).astype(BF16)


def ones_where(rows, labels):
    columns = labels.shape[1]
    return jnp.where(
        down_iota(rows, columns) == labels.astype(BF16), jnp.ones((), BF16), jnp.zeros((), BF16)
    )


def dot(a, b, transposed=False):
    return lax.dot_general(
        a, b, (((1,), (1 if transposed else 0,)), ((), ())), preferred_element_type=F32
    )


def gather_chunk(table, row, lane, weight):
    picks = jnp.concatenate([ones_where(128, lane[j : j + 1]) for j in range(4)], axis=1)
    found = dot(table, jnp.concatenate([picks, picks], axis=0))
    down = lax.broadcasted_iota(jnp.int32, (64, 128), 0).astype(F32)
    factors = [jnp.where(down == row[j : j + 1], weight[j : j + 1], 0.0) for j in range(4)]
    result = []
    for i in range(3):
        total = sum(
            factors[j] * found[64 * i : 64 * (i + 1), 128 * j : 128 * (j + 1)] for j in range(4)
        )
        result.append(jnp.sum(total, axis=0, keepdims=True))
    return jnp.concatenate(result, axis=0)


def scatter_chunk(row, lane, weight, traction):
    picks = jnp.concatenate([ones_where(128, lane[j : j + 1]) for j in range(4)], axis=1)
    rows = [ones_where(64, row[j : j + 1]) for j in range(4)]
    left = []
    parts = [
        [in_two(weight[j : j + 1] * traction[i : i + 1]) for j in range(4)] for i in range(3)
    ]
    for part in range(2):
        for i in range(3):
            left.append(
                jnp.concatenate([rows[j] * parts[i][j][part] for j in range(4)], axis=1)
            )
    return dot(jnp.concatenate(left, axis=0), picks, True)


def table_of(value):
    head, tail = in_two(value)
    return jnp.concatenate([head, tail], axis=1)


def gather_all(table, segments, bundle, mine, theirs, places, group):
    mine[...] = jnp.zeros_like(mine)

    def slave(k, _):
        at = pl.ds(pl.multiple_of(k * 128, 128), 128)
        block = segments[:, at]
        mine[0:3, at] = gather_chunk(table, block[8:12], block[12:16], block[0:4])
        return _

    lax.fori_loop(0, segments.shape[1] // 128, slave, 0)
    head, tail = in_two(mine[...])
    both = jnp.concatenate([head, tail], axis=0)
    target = segments[5:6, :]
    left = jnp.concatenate(
        [jnp.where(target == t, 1.0, 0.0).astype(BF16) * both for t in range(group)], axis=0
    )
    placed = dot(left, places[...], True).reshape(group, 16, CAP)
    theirs[...] = placed[:, 0:8] + placed[:, 8:16]

    def master(source, _):
        for half in range(CAP // 128):
            at = slice(128 * half, 128 * (half + 1))
            block = bundle[source, :, at]

            @pl.when(jnp.max(block[4:5]) > 0.0)
            def _work():
                theirs[source, 3:6, at] = gather_chunk(
                    table, block[8:12], block[12:16], block[0:4]
                )

        return _

    lax.fori_loop(0, group, master, 0)


def scatter_all(total, segments, bundle, mine, sent, arrived, places, pulls, group):
    head, tail = in_two(arrived[...].reshape(group * 8, CAP))
    returned = dot(
        jnp.concatenate([head, tail], axis=1), jnp.concatenate([places[...], places[...]], axis=0)
    )
    target = segments[5:6, :]
    back = sum(
        jnp.where(target == t, 1.0, 0.0) * returned[8 * t : 8 * (t + 1)] for t in range(group)
    )
    pulls[0:3, :] = segments[4:5, :] * (mine[0:3, :] - back[3:6, :])
    total[...] = jnp.zeros_like(total)

    def slave(k, _):
        at = pl.ds(pl.multiple_of(k * 128, 128), 128)
        block = segments[:, at]
        total[...] += scatter_chunk(block[8:12], block[12:16], block[0:4], pulls[0:3, at])
        return _

    lax.fori_loop(0, segments.shape[1] // 128, slave, 0)

    def master(source, _):
        for half in range(CAP // 128):
            at = slice(128 * half, 128 * (half + 1))
            block = bundle[source, :, at]

            @pl.when(jnp.max(block[4:5]) > 0.0)
            def _work():
                traction = block[4:5] * (sent[source, 3:6, at] - arrived[source, 0:3, at])
                total[...] += scatter_chunk(block[8:12], block[12:16], block[0:4], traction)

        return _

    lax.fori_loop(0, group, master, 0)


def swap_lanes(forth):
    a = lax.broadcasted_iota(jnp.int32, (128, 128), 0 if forth else 1)
    b = lax.broadcasted_iota(jnp.int32, (128, 128), 1 if forth else 0)
    return jnp.where(b == (a % 2) * 64 + a // 2, 1.0, 0.0).astype(F32)


def exact_dot(a, b):
    return lax.dot_general(
        a,
        b,
        (((1,), (0,)), ((), ())),
        precision=lax.Precision.HIGHEST,
        preferred_element_type=F32,
    )


def prepare_kernel(
    group,
    seed,
    modulus,
    mass,
    pair,
    slave_nodes,
    slave_weights,
    master_nodes,
    master_weights,
    penalty,
    own,
    message,
    packed,
    segments,
    places,
    swapped,
):
    swap = swap_lanes(True)
    for i in range(3):
        swapped[i] = exact_dot(seed[i].reshape(64, 128), swap).reshape(8, 8, 128)
    swapped[3] = exact_dot(mass[...].reshape(64, 128), swap).reshape(8, 8, 128)
    swapped[4] = exact_dot(modulus[...].reshape(64, 128), swap).reshape(8, 8, 128)
    for array in range(5):
        for x in range(8):
            for py in range(2):
                row = array * 64 + (x % 2 * 2 + py) * 16 + x // 2 * 4
                own[pl.ds(row, 4), :] = swapped[array, x, pl.ds(py, 4, stride=2), :]
    pack_halo(FIRST_PLAN, own, message)

    def place_of(node):
        x, y, z = node // 1024, node // 128 % 8, node % 128
        row = (x % 2 * 2 + y % 2) * 16 + x // 2 * 4 + y // 2
        return row.astype(F32), (z % 2 * 64 + z // 2).astype(F32)

    slave_row, slave_lane = place_of(slave_nodes[...])
    master_row, master_lane = place_of(master_nodes[...])
    target = pair[...].astype(F32)
    count = target.shape[1]
    chosen = ones_where(group, target)
    a = lax.broadcasted_iota(jnp.int32, (128, 128), 0)
    b = lax.broadcasted_iota(jnp.int32, (128, 128), 1)
    before = jnp.where(a < b, 1.0, 0.0).astype(BF16)
    ranks, base = [], jnp.zeros((group, 1), F32)
    for k in range(count // 128):
        part = chosen[:, 128 * k : 128 * (k + 1)]
        wide = part.astype(F32)
        rank = dot(part, before) + base
        ranks.append(jnp.sum(rank * wide, axis=0, keepdims=True))
        base = base + jnp.sum(wide, axis=1, keepdims=True)
    position = jnp.concatenate(ranks, axis=1)
    segments[0:4, :] = slave_weights[...]
    segments[4:5, :] = penalty[...]
    segments[5:6, :] = target
    segments[6:7, :] = position
    segments[7:8, :] = jnp.zeros_like(position)
    segments[8:12, :] = slave_row
    segments[12:16, :] = slave_lane
    spots = ones_where(CAP, position)
    places[...] = spots
    nothing = jnp.zeros((3, count), F32)
    values = jnp.concatenate([master_weights[...], penalty[...], nothing], axis=0)
    head, tail = in_two(values)
    nodes = jnp.concatenate([master_row, master_lane], axis=0)
    sent = jnp.concatenate([head, tail, nodes.astype(BF16), jnp.zeros((8, count), BF16)], axis=0)
    left = jnp.concatenate(
        [jnp.where(target == t, 1.0, 0.0).astype(BF16) * sent for t in range(group)], axis=0
    )
    placed = dot(left, spots, True).reshape(group, 32, CAP)
    packed[:, 0:8] = placed[:, 0:8] + placed[:, 8:16]
    packed[:, 8:16] = placed[:, 16:24]


def start_kernel(
    extents,
    own,
    message,
    bundle,
    segments,
    places,
    kept,
    wide_mod,
    mine,
    theirs,
    wide,
    wide_up,
    wide_mid,
    wide_mod_up,
    mass,
    diag,
):
    wide[...] = jnp.zeros_like(wide)
    mass[...] = jnp.zeros_like(mass)
    wide_mod[...] = jnp.zeros_like(wide_mod)
    for i in range(3):
        widen_own(own, i, wide, i)
    widen_own(own, 3, mass, 0)
    for x in range(4):
        wide_mod[pl.ds(8 * (x + 2) + 2, 4), :] = own[pl.ds(4 * 64 + 4 * x, 4), :]

    def store(array, parity, start, count, stride, value):
        at = rows_of(start, count, stride)
        if array < 3:
            wide[array, parity, at, :] = value
        elif array == 3:
            mass[0, parity, at, :] = value
        else:
            wide_mod[at, :] = value

    unpack_halo(FIRST_PLAN, extents, message, store)
    wide_mod_up[...] = shift_down(wide_mod[...])
    diagonal_into(diag, wide_mod, wide_mod_up)
    for i in range(3):
        for parity in range(4):
            entry = diag[i, parity] + mass[0, parity]
            inverse = jnp.where(mass[0, parity] > 0.0, 1.0 / entry, 0.0)
            diag[i, parity] = inverse
            wide[i, parity] = wide[i, parity] * inverse
        narrow(wide, i, kept, i)
        narrow(diag, i, kept, 3 + i)
    table = table_of(kept[0:192, :])
    gather_all(table, segments, bundle, mine, theirs, places, extents[1])
    lift(wide, wide_up, wide_mid)
    stiffness_into(diag, wide, wide_up, wide_mid, wide_mod, wide_mod_up)
    for i in range(3):
        narrow(diag, i, kept, 6 + i)
        at = pl.ds(64 * (6 + i), 64)
        kept[at, :] += own[pl.ds(192, 64), :] * kept[pl.ds(64 * i, 64), :]


def middle_kernel(
    extents,
    kept,
    bundle,
    segments,
    places,
    mine,
    sent,
    arrived,
    fields,
    message,
    mine_next,
    theirs,
    total,
    pulls,
):
    group = extents[1]
    scatter_all(total, segments, bundle, mine, sent, arrived, places, pulls, group)
    applied = kept[384:576, :] + total[0:192, :] + total[192:384, :]
    scaled = applied * kept[192:384, :]
    fields[0:192, :] = scaled
    fields[192:384, :] = applied
    pack_halo(NEXT_PLAN, fields, message)
    gather_all(table_of(scaled), segments, bundle, mine_next, theirs, places, group)


def end_kernel(
    extents,
    own,
    kept,
    fields,
    message,
    wide_mod,
    bundle,
    segments,
    places,
    mine,
    sent,
    arrived,
    last,
    sums,
    total,
    pulls,
    wide,
    wide_up,
    wide_mid,
    wide_mod_up,
    out,
):
    wide[...] = jnp.zeros_like(wide)
    for i in range(3):
        widen_own(fields, i, wide, i)

    def store(array, parity, start, count, stride, value):
        wide[array, parity, rows_of(start, count, stride), :] = value

    unpack_halo(NEXT_PLAN, extents, message, store)
    wide_mod_up[...] = shift_down(wide_mod[...])
    lift(wide, wide_up, wide_mid)
    stiffness_into(out, wide, wide_up, wide_mid, wide_mod, wide_mod_up)
    for i in range(3):
        narrow(out, i, last, i)
    scatter_all(total, segments, bundle, mine, sent, arrived, places, pulls, extents[1])
    scaled, applied = fields[0:192, :], fields[192:384, :]
    mass = own[192:256, :]
    again = (
        last[...]
        + jnp.concatenate([mass, mass, mass], axis=0) * scaled
        + total[0:192, :]
        + total[192:384, :]
    )
    last[...] = again
    direction = kept[0:192, :]

    def inner(a, b):
        return jnp.sum(a * b, axis=0, keepdims=True)

    sums[0:1, :] = inner(own[0:192, :], direction)
    sums[1:2, :] = inner(direction, applied)
    sums[2:3, :] = inner(scaled, applied)
    sums[3:4, :] = inner(scaled, again)
    sums[4:8, :] = jnp.zeros((4, 128), F32)


def finish_kernel(own, kept, fields, last, sums, adjoint, residual):
    totals = jnp.sum(sums[...], axis=1, keepdims=True)
    first, second, third, fourth = (totals[k : k + 1] for k in range(4))
    step = first / second
    later = step * step * third - first
    ratio = later / first
    grown = 1.0 + ratio
    curved = grown * grown * second - 2.0 * step * grown * third + step * step * fourth
    step_next = later / curved
    along = step + step_next * grown
    across = step_next * step
    swap = swap_lanes(False)
    found = along * kept[0:192, :] - across * fields[0:192, :]
    left = own[0:192, :] - along * fields[192:384, :] + across * last[...]
    for value, ref in ((found, adjoint), (left, residual)):
        value = exact_dot(value, swap)
        for i in range(3):
            for x in range(8):
                for py in range(2):
                    row = i * 64 + (x % 2 * 2 + py) * 16 + x // 2 * 4
                    ref[i, x, pl.ds(py, 4, stride=2), :] = value[row : row + 4]


def exchange_kernel(plan, extents, *refs):
    if plan:
        message, blocks, message_out, blocks_out = refs[:4]
        sends, receives, halo_sends, halo_receives, here = refs[4:]
    else:
        blocks, blocks_out, sends, receives, here = refs
    gx, gy = lax.axis_index("gx"), lax.axis_index("gy")
    wide, group = extents

    def beside(dx, dy):
        return lax.rem(gx + dx + wide, wide), lax.rem(gy + dy + group, group)

    barrier = pltpu.get_barrier_semaphore()
    peers = [(0, k) for k in range(1, group)]
    peers += [(dx, dy) for dx, dy, _, _, _ in plan if dx]
    for dx, dy in peers:
        pl.semaphore_signal(barrier, inc=1, device_id=beside(dx, dy), device_id_type=MESH)
    own = pltpu.make_async_copy(blocks.at[gy], blocks_out.at[gy], here)
    own.start()
    pl.semaphore_wait(barrier, len(peers))
    copies = []
    for k, (dx, dy, first, rows, _) in enumerate(plan):
        at = pl.ds(first, rows)
        copies.append(
            pltpu.make_async_remote_copy(
                src_ref=message.at[at],
                dst_ref=message_out.at[at],
                send_sem=halo_sends.at[k],
                recv_sem=halo_receives.at[k],
                device_id=beside(dx, dy),
                device_id_type=MESH,
            )
        )
        copies[-1].start()
    for k in range(1, group):
        target = beside(0, k)
        copies.append(
            pltpu.make_async_remote_copy(
                src_ref=blocks.at[target[1]],
                dst_ref=blocks_out.at[gy],
                send_sem=sends.at[k],
                recv_sem=receives.at[k],
                device_id=target,
                device_id_type=MESH,
            )
        )
        copies[-1].start()
    own.wait()
    for copy in copies:
        copy.wait()


def exchange(plan, extents, collective, message, blocks):
    outs = [jax.ShapeDtypeStruct(blocks.shape, F32)]
    args = [blocks]
    dma = pltpu.SemaphoreType.DMA
    scratch = [dma((extents[1],)), dma((extents[1],))]
    if plan:
        outs.insert(0, jax.ShapeDtypeStruct(message.shape, F32))
        args.insert(0, message)
        scratch += [dma((len(plan),)), dma((len(plan),))]
    scratch.append(dma)
    return pl.pallas_call(
        functools.partial(exchange_kernel, plan, extents),
        out_shape=outs,
        in_specs=[VMEM] * len(args),
        out_specs=[VMEM] * len(outs),
        scratch_shapes=scratch,
        compiler_params=pltpu.CompilerParams(
            collective_id=collective, has_side_effects=True, vmem_limit_bytes=LIMIT
        ),
        name=f"exchange_{collective}",
    )(*args)


def sum_kernel(extents, tile, out, across, along, middle, sends, receives):
    gx, gy = lax.axis_index("gx"), lax.axis_index("gy")
    wide, group = extents
    barrier = pltpu.get_barrier_semaphore()
    rows = [(lax.rem(gx + k, wide), gy) for k in range(1, wide)]
    columns = [(gx, lax.rem(gy + k, group)) for k in range(1, group)]
    for device in rows + columns:
        pl.semaphore_signal(barrier, inc=1, device_id=device, device_id_type=MESH)
    across[gx] = tile[...]
    pl.semaphore_wait(barrier, len(rows) + len(columns))

    def send(source, slots, me, devices, first):
        copies = []
        for k, device in enumerate(devices):
            copies.append(
                pltpu.make_async_remote_copy(
                    src_ref=source,
                    dst_ref=slots.at[me],
                    send_sem=sends.at[first + k],
                    recv_sem=receives.at[first + k],
                    device_id=device,
                    device_id_type=MESH,
                )
            )
            copies[-1].start()
        for copy in copies:
            copy.wait()

    send(tile, across, gx, rows, 0)
    part = jnp.sum(across[...], axis=0)
    middle[...] = part
    along[gy] = part
    send(middle, along, gy, columns, len(rows))
    out[...] = jnp.sum(along[...], axis=0)


def global_sum(extents, collective, tile):
    count = sum(extents)
    return pl.pallas_call(
        functools.partial(sum_kernel, extents),
        out_shape=jax.ShapeDtypeStruct(tile.shape, F32),
        in_specs=[VMEM],
        out_specs=VMEM,
        scratch_shapes=[
            pltpu.VMEM((extents[0],) + tile.shape, F32),
            pltpu.VMEM((extents[1],) + tile.shape, F32),
            pltpu.VMEM(tile.shape, F32),
            pltpu.SemaphoreType.DMA((count,)),
            pltpu.SemaphoreType.DMA((count,)),
        ],
        compiler_params=pltpu.CompilerParams(collective_id=collective, has_side_effects=True),
        name="global_sum",
    )(tile)


def local(body, outs, scratch, args, name):
    return pl.pallas_call(
        body,
        out_shape=[jax.ShapeDtypeStruct(shape, dtype) for shape, dtype in outs],
        in_specs=[VMEM] * len(args),
        out_specs=[VMEM] * len(outs),
        scratch_shapes=[pltpu.VMEM(shape, F32) for shape in scratch],
        compiler_params=pltpu.CompilerParams(vmem_limit_bytes=LIMIT),
        name=name,
    )(*args)


def shards(
    seed_grad,
    modulus,
    lumped_mass,
    pair_dest,
    slave_nodes,
    slave_weights,
    master_nodes,
    master_weights,
    penalty,
):
    extents = (lax.axis_size("gx"), lax.axis_size("gy"))
    group, count = extents[1], penalty.shape[0]
    parts = ((group, 8, CAP), F32)
    field = (3, 4, WIDE, 128)
    own, message, packed, segments, places = local(
        functools.partial(prepare_kernel, group),
        [
            ((320, 128), F32),
            ((FIRST_ROWS, 128), F32),
            ((group, 16, CAP), F32),
            ((16, count), F32),
            ((CAP, count), BF16),
        ],
        [(5, 8, 8, 128)],
        (
            seed_grad,
            modulus,
            lumped_mass,
            pair_dest.reshape(1, count),
            slave_nodes,
            slave_weights,
            master_nodes,
            master_weights,
            penalty.reshape(1, count),
        ),
        "prepare",
    )
    message, bundle = exchange(FIRST_PLAN, extents, 1, message, packed)
    kept, wide_mod, mine, theirs = local(
        functools.partial(start_kernel, extents),
        [((576, 128), F32), ((WIDE, 128), F32), ((8, count), F32), parts],
        [field, (3, 3, WIDE, 128), (3, WIDE, 128), (WIDE, 128), (1, 4, WIDE, 128), field],
        (own, message, bundle, segments, places),
        "start",
    )
    (arrived,) = exchange([], extents, 2, None, theirs)
    fields, message, mine_next, theirs_next = local(
        functools.partial(middle_kernel, extents),
        [((384, 128), F32), ((NEXT_ROWS, 128), F32), ((8, count), F32), parts],
        [(384, 128), (8, count)],
        (kept, bundle, segments, places, mine, theirs, arrived),
        "middle",
    )
    message, arrived = exchange(NEXT_PLAN, extents, 3, message, theirs_next)
    last, sums = local(
        functools.partial(end_kernel, extents),
        [((192, 128), F32), ((8, 128), F32)],
        [
            (384, 128),
            (8, count),
            field,
            (3, 3, WIDE, 128),
            (3, WIDE, 128),
            (WIDE, 128),
            field,
        ],
        (
            own,
            kept,
            fields,
            message,
            wide_mod,
            bundle,
            segments,
            places,
            mine_next,
            theirs_next,
            arrived,
        ),
        "end",
    )
    sums = global_sum(extents, 4, sums)
    return tuple(
        local(
            finish_kernel,
            [(seed_grad.shape, F32), (seed_grad.shape, F32)],
            [],
            (own, kept, fields, last, sums),
            "finish",
        )
    )


def solution(mesh):
    placed = (
        P(None, "gx", "gy", None),
        P("gx", "gy", None),
        P("gx", "gy", None),
        P(("gx", "gy"), None),
        P(None, ("gx", "gy")),
        P(None, ("gx", "gy")),
        P(None, ("gx", "gy")),
        P(None, ("gx", "gy")),
        P(("gx", "gy")),
    )
    return jax.shard_map(
        shards,
        mesh=mesh,
        in_specs=placed,
        out_specs=(P(None, "gx", "gy", None), P(None, "gx", "gy", None)),
        check_vma=False,
    )
```

time: 2080 us -> 115 us (0.06)
  other arithmetic: 1410 us -> 0 us
  local copies, waits for them, and re-layouts: 385 us -> 7.91 us
  blocking collectives: 200 us -> 0 us
  Pallas kernels: 0 us -> 106 us
  starting transfers between devices: 61.3 us -> 0 us
    unnamed x77 -> x0, other arithmetic: 1090 us -> none
    scatter-add x4 -> x0, other arithmetic: 273 us -> none  [the longest x2 223 us: shards(): result.at[:, far_nodes]]
    psum x3 -> x0, blocking collectives: 200 us -> none  [global_dot(): return lax.psum(jnp.sum(first_vec * second_vec), ('gx', 'gy'))]
    gather x6 -> x0, local copies, waits for them, and re-layouts: 147 us -> none  [the longest x2 113 us: shards(): flattened[:, far_nodes] * far_weights[None]]
    pallas_call x0 -> x9, Pallas kernels: none -> 106 us  [the longest x5 57.3 us: local(): pl.pallas_call(body, out_shape=[jax.ShapeDtypeStruct(shape, dtype) for sh...]
    slice x65 -> x0, local copies, waits for them, and re-layouts: 105 us -> none  [the longest x40 88.9 us: gather_nodes(): padded[:, strided(o[0], counts[0]), strided(o[1], counts[1]), strided(o[2...]
    squeeze x120 -> x0, local copies, waits for them, and re-layouts: 71.6 us -> none  [spread_nodes(): values[n]]
    ppermute x12 -> x0, starting transfers between devices: 31.2 us -> none  [the longest x6 21.2 us: with_halo(): lax.ppermute(lax.slice_in_dim(block, block.shape[dim] - width, None, axis...]
  transfers between devices with their start and end apart: 16 -> 0, of which waited for: 0 -> 0; matrix products, arithmetic and copies ran while one was open for 47% -> 0% of each run, Pallas kernels for 0% -> 0%
where the time goes in v1:
time: 115 us
  Pallas kernels  106 us (92%)
  local copies, waits for them, and re-layouts  7.91 us (7%)
    pallas_call x5, Pallas kernels, local(): pl.pallas_call(body, out_shape=[jax.ShapeDtypeStruct(shape, dtype) for sh...  57.3 us
    pallas_call x3, Pallas kernels, exchange(): pl.pallas_call(functools.partial(exchange_kernel, plan, extents), out_sha...  33.4 us
    pallas_call x1, Pallas kernels, global_sum(): pl.pallas_call(functools.partial(sum_kernel, extents), out_shape=jax.Shap...  15.3 us
    unnamed x22, local copies, waits for them, and re-layouts  7.91 us

profile of v1, /device:TPU:1, one launch (start us, length us, event | category | flops | bytes accessed | tf_op | source)
XLA Modules:
  0.0 114.6 jit_solution(1300481834886088702)
XLA Ops:
  0.6 0.0 copy-start
  0.6 0.9 copy-done
  1.5 0.0 copy-start.1
  1.5 0.8 copy-done.1
  2.3 0.0 copy-start.2
  2.3 0.8 copy-done.2
  3.0 0.0 copy-start.4
  3.0 0.7 copy-done.4
  3.8 0.0 copy-start.5
  3.8 0.7 copy-done.5
  4.5 0.0 copy-start.6
  4.5 0.7 copy-done.6
  5.2 0.0 copy-start.7
  5.2 0.7 copy-done.7
  5.9 0.0 copy-start.9
  5.9 0.7 copy-done.9
  6.6 0.0 copy-start.10
  6.6 0.7 copy-done.10
  7.3 1.0 prepare.1
  8.3 13.3 %exchange_1.1 = (f32[288,128]{1,0:T(8,128)S(1)}, f32[16,16,256]{2,1,0:T(8,128)S(1)}) custom-call(f32[288,128]{1,0:T(8,128)S(1)} %get-tuple-element.22.refs_0_, f32[16,16,256]{2,1,0:T(8,128)S(1)} %get-tuple-element.23.refs_1_), custom_call_target="tpu_custom_call" | custom-call | tf_op jit(solution)/shard_map/exchange_1/pallas_call | solution.py:820
  21.5 14.1 %start.1 = (f32[576,128]{1,0:T(8,128)S(1)}, f32[72,128]{1,0:T(8,128)S(1)}, f32[8,1024]{1,0:T(8,128)S(1)}, f32[16,8,256]{2,1,0:T(8,128)S(1)}) custom-call(f32[320,128]{1,0:T(8,128)S(1)} %get-tuple-element.21.own, f32[288,128]{1,0:T(8,128)S(1)} %get-tuple-element.24.message, f32[16,16,256]{2,1,0:T(8,128)S(1)} %get-tuple-element.25.bundle, ...), custom_call_target="tpu_custom_call" | custom-call | tf_op jit(solution)/shard_map/start/pallas_call | solution.py:889
  35.6 7.2 %exchange_2.1.arrived = f32[16,8,256]{2,1,0:T(8,128)S(1)} custom-call(f32[16,8,256]{2,1,0:T(8,128)S(1)} %get-tuple-element.30.refs_0_.sent), custom_call_target="tpu_custom_call" | custom-call | tf_op jit(solution)/shard_map/exchange_2/pallas_call | solution.py:820
  42.8 26.2 %middle.1 = (f32[384,128]{1,0:T(8,128)S(1)}, f32[184,128]{1,0:T(8,128)S(1)}, f32[8,1024]{1,0:T(8,128)S(1)}, f32[16,8,256]{2,1,0:T(8,128)S(1)}) custom-call(f32[576,128]{1,0:T(8,128)S(1)} %get-tuple-element.28.kept, f32[16,16,256]{2,1,0:T(8,128)S(1)} %get-tuple-element.25.bundle, f32[16,1024]{1,0:T(8,128)S(1)} %get-tuple-element.26.segments, ...), custom_call_target="tpu_custom_call" | custom-call | tf_op jit(solution)/shard_map/middle/pallas_call | solution.py:889
  69.1 12.9 %exchange_3.1 = (f32[184,128]{1,0:T(8,128)S(1)}, f32[16,8,256]{2,1,0:T(8,128)S(1)}) custom-call(f32[184,128]{1,0:T(8,128)S(1)} %get-tuple-element.32.refs_0_, f32[16,8,256]{2,1,0:T(8,128)S(1)} %get-tuple-element.33.refs_1_.sent), custom_call_target="tpu_custom_call" | custom-call | tf_op jit(solution)/shard_map/exchange_3/pallas_call | solution.py:820
  82.0 14.9 %end.1 = (f32[192,128]{1,0:T(8,128)S(1)}, f32[8,128]{1,0:T(8,128)S(1)}) custom-call(f32[320,128]{1,0:T(8,128)S(1)} %get-tuple-element.21.own, f32[576,128]{1,0:T(8,128)S(1)} %get-tuple-element.28.kept, f32[384,128]{1,0:T(8,128)S(1)} %get-tuple-element.31.fields, f32[184,128]{1,0:T(8,128)S(1)} %get-tuple-element.34.message, ...), custom_call_target="tpu_custom_call" | custom-call | tf_op jit(solution)/shard_map/end/pallas_call | solution.py:889
  96.9 0.0 copy-start.8
  96.9 0.6 copy-done.8
  97.5 15.3 %global_sum.1.sums = f32[8,128]{1,0:T(8,128)} custom-call(f32[8,128]{1,0:T(8,128)} %copy-done.8), custom_call_target="tpu_custom_call" | custom-call | tf_op jit(solution)/shard_map/global_sum/pallas_call | solution.py:871
  112.8 0.0 copy-start.3
  112.8 0.7 copy-done.3
  113.4 1.1 finish.1
Async XLA Ops:
  0.6 0.9 copy-start
  1.5 0.8 copy-start.1
  2.3 0.8 copy-start.2
  3.0 0.7 copy-start.4
  3.8 0.7 copy-start.5
  4.5 0.7 copy-start.6
  5.2 0.7 copy-start.7
  5.9 0.7 copy-start.9
  6.6 0.7 copy-start.10
  96.9 0.6 copy-start.8
  112.8 0.7 copy-start.3

commit v2 on v1

v2 whole, which is shorter than its diff:
```python
import functools
import math

import jax
import jax.numpy as jnp
import numpy as np
from jax import lax
from jax.experimental import pallas as pl
from jax.experimental.pallas import tpu as pltpu
from jax.sharding import PartitionSpec as P

CAP = 256
SHEAR = 1.0 / 2.6
LAME = 0.3 / 0.52
MESH = pl.DeviceIdType.MESH
F32 = jnp.float32
BF16 = jnp.bfloat16
VMEM = pl.BlockSpec(memory_space=pltpu.VMEM)
LIMIT = 64 * 1024 * 1024

WIDE = 72


def shape_tables():
    abscissa = 1.0 / math.sqrt(3.0)
    points = [
        (a, b, c)
        for a in (-abscissa, abscissa)
        for b in (-abscissa, abscissa)
        for c in (-abscissa, abscissa)
    ]
    offsets = [
        (i, j, k)
        for i in range(3)
        for j in range(3)
        for k in range(3)
        if (i == 1) + (j == 1) + (k == 1) <= 1
    ]
    derivative = np.zeros((8, 3, 20))
    for g, location in enumerate(points):
        for n, offset in enumerate(offsets):
            natural = [offset[d] - 1 for d in range(3)]
            factors = [
                1.0 - location[d] ** 2 if natural[d] == 0 else 1.0 + location[d] * natural[d]
                for d in range(3)
            ]
            slopes = [
                -2.0 * location[d] if natural[d] == 0 else float(natural[d]) for d in range(3)
            ]
            linear = sum(location[d] * natural[d] for d in range(3)) - 2.0
            for d in range(3):
                others = factors[(d + 1) % 3] * factors[(d + 2) % 3]
                if 0 in natural:
                    derivative[g, d, n] = slopes[d] * others / 4.0
                else:
                    derivative[g, d, n] = natural[d] * others * (linear + factors[d]) / 8.0
    return derivative, offsets


def signs(count, dims):
    table = np.ones((count, count))
    for t in range(count):
        for c in range(count):
            for d in range(dims):
                if t >> d & 1 and not c >> d & 1:
                    table[t, c] = -table[t, c]
    return table


def element_tables():
    derivative, offsets = shape_tables()
    eight, four = signs(8, 3), signs(4, 2)
    modal = np.einsum("sg,gan->asn", eight, derivative) / 8.0
    corner_at = [offsets.index((c >> 2 << 1, (c >> 1 & 1) << 1, (c & 1) << 1)) for c in range(8)]
    edge_at = []
    for d in range(3):
        row = []
        for c in range(4):
            offset = [(c >> 1) << 1, (c & 1) << 1]
            offset.insert(d, 1)
            row.append(offsets.index(tuple(offset)))
        edge_at.append(row)
    corner_terms = np.einsum("tn,asn->ast", eight, modal[:, :, corner_at]) / 8.0
    edge_terms = [np.einsum("tn,asn->ast", four, modal[:, :, edge_at[d]]) / 4.0 for d in range(3)]
    trilinear = np.array([(1.0 / math.sqrt(3.0)) ** bin(t).count("1") / 8.0 for t in range(8)])
    at_points = np.einsum("t,tg->gt", trilinear, eight)
    squares = derivative * derivative
    weight = np.einsum(
        "gt,gni->tni",
        at_points,
        SHEAR * squares.sum(axis=1)[:, :, None] + (LAME + SHEAR) * np.swapaxes(squares, 1, 2),
    )
    corner_diag = np.einsum("un,tni->uti", eight, weight[:, corner_at]) / 8.0
    edge_diag = [np.einsum("un,tni->uti", four, weight[:, edge_at[d]]) / 4.0 for d in range(3)]
    return corner_terms, edge_terms, trilinear, corner_diag, edge_diag


def split_sums(values):
    values = list(values)
    step = 1
    while step < len(values):
        for low in range(len(values)):
            if not low & step:
                a, b = values[low], values[low | step]
                values[low], values[low | step] = b + a, b - a
        step *= 2
    return values


def join_sums(values):
    values = list(values)
    step = 1
    while step < len(values):
        for low in range(len(values)):
            if not low & step:
                a, b = values[low], values[low | step]
                values[low], values[low | step] = a - b, a + b
        step *= 2
    return values


def combine(terms):
    total = None
    for factor, value in terms:
        if abs(factor) < 1e-12:
            continue
        term = value * np.float32(factor)
        total = term if total is None else total + term
    return total


def lanes(rows):
    return lax.broadcasted_iota(jnp.int32, (rows, 128), 1)


def shift_down(value):
    return jnp.where(lanes(value.shape[0]) == 63, 0.0, pltpu.roll(value, 127, 1))


def collect(low, middle, high):
    total = low + jnp.where(lanes(8) < 64, pltpu.roll(high, 1, 1), 0.0)
    if middle is not None:
        total = total + pltpu.roll(middle, 64, 1)
    return total


def corner_moduli(wide_mod, wide_mod_up, group):
    values = []
    for c in range(8):
        ref = wide_mod_up if c & 1 else wide_mod
        values.append(ref[pl.ds(8 * (group + (c >> 2)) + (c >> 1 & 1), 8), :])
    inside = lanes(8) < 64
    return split_sums([jnp.where(inside, value, 0.0) for value in values])


def edge_corner(d, c):
    where = [c >> 1, c & 1]
    where.insert(d, None)
    return where


def add_rows(ref, index, row, value):
    ref[index + (pl.ds(row, 8), slice(None))] += value


def scatter_forces(out, i, corner, edges, group):
    for xy in range(4):
        row = 8 * (group + (xy >> 1)) + (xy & 1)
        add_rows(out, (i, 0), row, collect(corner[2 * xy], edges[2][xy], corner[2 * xy + 1]))
    for y in range(2):
        add_rows(out, (i, 2), 8 * group + y, collect(edges[0][2 * y], None, edges[0][2 * y + 1]))
    for x in range(2):
        add_rows(
            out, (i, 1), 8 * (group + x), collect(edges[1][2 * x], None, edges[1][2 * x + 1])
        )


def diagonal_into(out, wide_mod, wide_mod_up):
    corner_diag, edge_diag = element_tables()[3:]
    out[...] = jnp.zeros_like(out)
    for group in range(7):
        moduli = corner_moduli(wide_mod, wide_mod_up, group)
        for i in range(3):
            corner = join_sums(
                [
                    combine([(corner_diag[u, t, i], moduli[t]) for t in range(8)])
                    for u in range(8)
                ]
            )
            edges = [
                join_sums(
                    [
                        combine([(edge_diag[d][u, t, i], moduli[t]) for t in range(8)])
                        for u in range(4)
                    ]
                )
                for d in range(3)
            ]
            scatter_forces(out, i, corner, edges, group)


def stiffness_into(out, wide, wide_up, wide_mid, wide_mod, wide_mod_up):
    corner_terms, edge_terms, trilinear = element_tables()[:3]
    out[...] = jnp.zeros_like(out)
    for group in range(1, 6):
        moduli = corner_moduli(wide_mod, wide_mod_up, group)
        points = join_sums([moduli[t] * np.float32(trilinear[t]) for t in range(8)])
        slopes = []
        for i in range(3):
            corner = []
            for c in range(8):
                ref = wide_up if c & 1 else wide
                corner.append(ref[i, 0, pl.ds(8 * (group + (c >> 2)) + (c >> 1 & 1), 8), :])
            corner = split_sums(corner)
            edges = []
            for d in range(3):
                values = []
                for c in range(4):
                    x, y, z = edge_corner(d, c)
                    row = 8 * (group + (x or 0)) + (y or 0)
                    parity = (2, 1, 0)[d]
                    if d == 2:
                        values.append(wide_mid[i, pl.ds(row, 8), :])
                    else:
                        values.append((wide_up if z else wide)[i, parity, pl.ds(row, 8), :])
                edges.append(split_sums(values))
            slopes.append(
                [
                    [
                        combine(
                            [(corner_terms[a, s, t], corner[t]) for t in range(8)]
                            + [
                                (edge_terms[d][a, s, t], edges[d][t])
                                for d in range(3)
                                for t in range(4)
                            ]
                        )
                        for s in range(8)
                    ]
                    for a in range(3)
                ]
            )

        def plus(a, b):
            return a if b is None else b if a is None else a + b

        zero = jnp.zeros((8, 128), F32)
        strain = {}
        for a in range(3):
            strain[a, a] = slopes[a][a]
            for b in range(a):
                strain[b, a] = [plus(p, q) for p, q in zip(slopes[a][b], slopes[b][a])]
        strain = {
            key: join_sums([zero if v is None else v for v in value])
            for key, value in strain.items()
        }
        stress = {key: [] for key in strain}
        for g in range(8):
            volume = (strain[0, 0][g] + strain[1, 1][g] + strain[2, 2][g]) * np.float32(LAME)
            for a in range(3):
                stress[a, a].append(
                    points[g] * (volume + strain[a, a][g] * np.float32(2.0 * SHEAR))
                )
            scaled = points[g] * np.float32(SHEAR)
            for key in ((0, 1), (0, 2), (1, 2)):
                stress[key].append(scaled * strain[key][g])
        stress = {key: split_sums(value) for key, value in stress.items()}
        for i in range(3):
            pairs = [
                (a, s, stress[min(a, i), max(a, i)][s]) for a in range(3) for s in range(8)
            ]
            corner = join_sums(
                [combine([(corner_terms[a, s, t], v) for a, s, v in pairs]) for t in range(8)]
            )
            edges = [
                join_sums(
                    [combine([(edge_terms[d][a, s, t], v) for a, s, v in pairs]) for t in range(4)]
                )
                for d in range(3)
            ]
            scatter_forces(out, i, corner, edges, group)


def lift(wide, wide_up, wide_mid):
    for i in range(3):
        for parity in range(3):
            wide_up[i, parity] = shift_down(wide[i, parity])
        wide_mid[i] = pltpu.roll(wide[i, 0], 64, 1)


def halo_plan(fields, with_modulus):
    plan, first = [], 0
    for dx in (-1, 0, 1):
        for dy in (-1, 0, 1):
            if dx == 0 and dy == 0:
                continue
            pieces = []

            def places(step, both):
                if step == 1:
                    return [(p, 3, 1) for p in ((0, 1) if both else (0,))]
                return [(0, 0, 6)]

            def strips(array, xs, ys):
                for px, ox, wx in xs:
                    for py, oy, wy in ys:
                        if ox is None:
                            pieces.append((array, px * 2 + py, oy, 4, 4, 8 * 2 + wy, 8))
                        elif oy is None:
                            pieces.append((array, px * 2 + py, 4 * ox, 4, 1, 8 * wx + 2, 1))
                        else:
                            pieces.append((array, px * 2 + py, 4 * ox + oy, 1, 1, 8 * wx + wy, 1))

            every = [(0, None, None), (1, None, None)]
            for array in range(fields):
                strips(
                    array,
                    every if dx == 0 else places(dx, True),
                    every if dy == 0 else places(dy, True),
                )
            if with_modulus:
                deep = {1: [(0, 3, 1), (0, 2, 0)], -1: [(0, 0, 6), (0, 1, 7)], 0: every[:1]}
                strips(fields, deep[dx], deep[dy])
            rows = sum(piece[3] for piece in pieces)
            plan.append((dx, dy, first, -(-rows // 8) * 8, pieces))
            first += plan[-1][3]
    return plan, first


FIRST_PLAN, FIRST_ROWS = halo_plan(4, True)
NEXT_PLAN, NEXT_ROWS = halo_plan(3, False)


def rows_of(start, count, stride):
    return pl.ds(start, count) if stride == 1 else pl.ds(start, count, stride=stride)


def pack_halo(plan, own, message):
    message[...] = jnp.zeros_like(message)
    for _, _, first, _, pieces in plan:
        at = first
        for array, parity, start, count, stride, _, _ in pieces:
            source = own[rows_of(array * 64 + parity * 16 + start, count, stride), :]
            message[pl.ds(at, count), :] = source
            at += count


def unpack_halo(plan, extents, message, store):
    gx, gy = lax.axis_index("gx"), lax.axis_index("gy")
    for dx, dy, first, _, pieces in plan:
        inside = None
        for step, at, extent in ((dx, gx, extents[0]), (dy, gy, extents[1])):
            if step:
                here = at > 0 if step == 1 else at < extent - 1
                inside = here if inside is None else jnp.logical_and(inside, here)
        keep = jnp.where(inside, 1.0, 0.0).astype(F32)
        at = first
        for array, parity, _, count, _, start, stride in pieces:
            store(array, parity, start, count, stride, message[pl.ds(at, count), :] * keep)
            at += count


def widen_own(own, array, wide, i):
    for parity in range(4):
        for x in range(4):
            wide[i, parity, pl.ds(8 * (x + 2) + 2, 4), :] = own[
                pl.ds(array * 64 + parity * 16 + 4 * x, 4), :
            ]


def narrow(wide, i, own, array):
    for parity in range(4):
        for x in range(4):
            own[pl.ds(array * 64 + parity * 16 + 4 * x, 4), :] = wide[
                i, parity, pl.ds(8 * (x + 2) + 2, 4), :
            ]


def in_two(value):
    head = value.astype(BF16)
    return head, (value - head.astype(F32)).astype(BF16)


def down_iota(rows, columns):
    return lax.broadcasted_iota(jnp.int32, (rows, columns), 0).astype(F32).astype(BF16)


def ones_where(rows, labels):
    columns = labels.shape[1]
    return jnp.where(
        down_iota(rows, columns) == labels.astype(BF16), jnp.ones((), BF16), jnp.zeros((), BF16)
    )


def dot(a, b, transposed=False):
    return lax.dot_general(
        a, b, (((1,), (1 if transposed else 0,)), ((), ())), preferred_element_type=F32
    )


BLOCK = CAP


def picks_of(lane, extent):
    return jnp.concatenate([ones_where(extent, lane[j : j + 1]) for j in range(4)], axis=1)


def gather_block(table, block):
    count = block.shape[1]
    picks = picks_of(block[12:16], 128)
    found = dot(table, jnp.concatenate([picks, picks], axis=0))
    down = lax.broadcasted_iota(jnp.int32, (64, count), 0).astype(F32)
    factors = [
        jnp.where(down == block[8 + j : 9 + j], block[j : j + 1], 0.0) for j in range(4)
    ]
    result = []
    for i in range(3):
        total = sum(
            factors[j] * found[64 * i : 64 * (i + 1), count * j : count * (j + 1)]
            for j in range(4)
        )
        result.append(jnp.sum(total, axis=0, keepdims=True))
    return jnp.concatenate(result, axis=0)


def scatter_block(block, traction):
    upper = jnp.where(block[8:12] >= 32.0, 1.0, 0.0)
    row, lane = block[8:12] - 32.0 * upper, block[12:16] + 128.0 * upper
    rows = [ones_where(32, row[j : j + 1]) for j in range(4)]
    parts = [
        [in_two(block[j : j + 1] * traction[i : i + 1]) for j in range(4)] for i in range(3)
    ]
    left = [
        jnp.concatenate([rows[j] * parts[i][j][part] for j in range(4)], axis=1)
        for part in range(2)
        for i in range(3)
    ]
    return dot(jnp.concatenate(left, axis=0), picks_of(lane, 256), True)


def total_rows(total):
    value = total[0:96, :] + total[96:192, :]
    return jnp.concatenate(
        [
            value[32 * i : 32 * (i + 1), 128 * half : 128 * (half + 1)]
            for i in range(3)
            for half in range(2)
        ],
        axis=0,
    )


def table_of(value):
    head, tail = in_two(value)
    return jnp.concatenate([head, tail], axis=1)


def each(first, last, body, unroll):
    def step(k, carry):
        body(k)
        return carry

    lax.fori_loop(first, last, step, 0, unroll=unroll)


def gather_slaves(table, segments, mine, theirs, places, group):
    mine[...] = jnp.zeros_like(mine)

    def slave(k):
        at = pl.ds(pl.multiple_of(k * BLOCK, BLOCK), BLOCK)
        mine[0:3, at] = gather_block(table, segments[:, at])

    each(0, segments.shape[1] // BLOCK, slave, 4)
    head, tail = in_two(mine[...])
    both = jnp.concatenate([head, tail], axis=0)
    target = segments[5:6, :]
    left = jnp.concatenate(
        [jnp.where(target == t, 1.0, 0.0).astype(BF16) * both for t in range(group)], axis=0
    )
    placed = dot(left, places[...], True).reshape(group, 16, CAP)
    theirs[...] = placed[:, 0:8] + placed[:, 8:16]


def gather_masters(table, bundle, theirs, group):
    theirs[...] = jnp.zeros_like(theirs)

    def master(source):
        theirs[source, 0:3, :] = gather_block(table, bundle[source])

    each(0, group, master, 8)


def pull_slaves(segments, mine, returned, places, pulls, group):
    head, tail = in_two(returned[...].reshape(group * 8, CAP))
    found = dot(
        jnp.concatenate([head, tail], axis=1),
        jnp.concatenate([places[...], places[...]], axis=0),
    )
    target = segments[5:6, :]
    back = sum(jnp.where(target == t, 1.0, 0.0) * found[8 * t : 8 * (t + 1)] for t in range(group))
    gap = mine[0:3, :] - back[0:3, :]
    pulls[0:3, :] = segments[4:5, :] * gap
    return gap


def scatter_slaves(total, segments, pulls):
    def slave(k):
        at = pl.ds(pl.multiple_of(k * 2 * BLOCK, 2 * BLOCK), 2 * BLOCK)
        total[...] += scatter_block(segments[:, at], pulls[0:3, at])

    each(0, segments.shape[1] // (2 * BLOCK), slave, 2)


def scatter_masters(total, bundle, sent, arrived, first, last):
    def master(k):
        pair = [2 * k, 2 * k + 1]
        block = jnp.concatenate([bundle[source] for source in pair], axis=1)
        gap = [sent[source, 0:3, :] - arrived[source, 0:3, :] for source in pair]
        total[...] += scatter_block(block, block[4:5] * jnp.concatenate(gap, axis=1))

    each(first // 2, last // 2, master, 4)


def swap_lanes(forth):
    a = lax.broadcasted_iota(jnp.int32, (128, 128), 0 if forth else 1)
    b = lax.broadcasted_iota(jnp.int32, (128, 128), 1 if forth else 0)
    return jnp.where(b == (a % 2) * 64 + a // 2, 1.0, 0.0).astype(F32)


def reorder(value, forth):
    head = value.astype(BF16)
    rest = value - head.astype(F32)
    middle = rest.astype(BF16)
    tail = (rest - middle.astype(F32)).astype(BF16)
    swap = swap_lanes(forth).astype(BF16)
    return dot(
        jnp.concatenate([head, middle, tail], axis=1), jnp.concatenate([swap, swap, swap], axis=0)
    )


def lay_out(seed, modulus, mass, own, swapped):
    values = [seed[...].reshape(192, 128), mass[...].reshape(64, 128)]
    values.append(modulus[...].reshape(64, 128))
    swapped[...] = reorder(jnp.concatenate(values, axis=0), True).reshape(5, 8, 8, 128)
    for array in range(5):
        for x in range(8):
            for py in range(2):
                row = array * 64 + (x % 2 * 2 + py) * 16 + x // 2 * 4
                own[pl.ds(row, 4), :] = swapped[array, x, pl.ds(py, 4, stride=2), :]


def place_of(node):
    x, y, z = node // 1024, node // 128 % 8, node % 128
    row = (x % 2 * 2 + y % 2) * 16 + x // 2 * 4 + y // 2
    return row.astype(F32), (z % 2 * 64 + z // 2).astype(F32)


def place_segments(
    group,
    pair,
    slave_nodes,
    slave_weights,
    master_nodes,
    master_weights,
    penalty,
    packed,
    segments,
    places,
):
    slave_row, slave_lane = place_of(slave_nodes[...])
    master_row, master_lane = place_of(master_nodes[...])
    target = pair[...].astype(F32)
    count = target.shape[1]
    chosen = ones_where(group, target)
    a = lax.broadcasted_iota(jnp.int32, (128, 128), 0)
    b = lax.broadcasted_iota(jnp.int32, (128, 128), 1)
    before = jnp.where(a < b, 1.0, 0.0).astype(BF16)
    ranks, base = [], jnp.zeros((group, 1), F32)
    for k in range(count // 128):
        part = chosen[:, 128 * k : 128 * (k + 1)]
        wide = part.astype(F32)
        rank = dot(part, before) + base
        ranks.append(jnp.sum(rank * wide, axis=0, keepdims=True))
        base = base + jnp.sum(wide, axis=1, keepdims=True)
    position = jnp.concatenate(ranks, axis=1)
    segments[0:4, :] = slave_weights[...]
    segments[4:5, :] = penalty[...]
    segments[5:6, :] = target
    segments[6:7, :] = position
    segments[7:8, :] = jnp.zeros_like(position)
    segments[8:12, :] = slave_row
    segments[12:16, :] = slave_lane
    spots = ones_where(CAP, position)
    places[...] = spots
    nothing = jnp.zeros((3, count), F32)
    values = jnp.concatenate([master_weights[...], penalty[...], nothing], axis=0)
    head, tail = in_two(values)
    nodes = jnp.concatenate([master_row, master_lane], axis=0)
    sent = jnp.concatenate([head, tail, nodes.astype(BF16), jnp.zeros((8, count), BF16)], axis=0)
    left = jnp.concatenate(
        [jnp.where(target == t, 1.0, 0.0).astype(BF16) * sent for t in range(group)], axis=0
    )
    placed = dot(left, spots, True).reshape(group, 32, CAP)
    packed[:, 0:8] = placed[:, 0:8] + placed[:, 8:16]
    packed[:, 8:16] = placed[:, 16:24]


def inner(a, b):
    return jnp.sum(a * b, axis=0, keepdims=True)


INPUTS = (
    "seed",
    "modulus",
    "mass",
    "pair",
    "slave_nodes",
    "slave_weights",
    "master_nodes",
    "master_weights",
    "penalty",
)


def scratch_of(extents, args):
    group, count = extents[1], args[-1].shape[-1]
    dma, parts, field = pltpu.SemaphoreType.DMA, (group, 8, CAP), (3, 4, WIDE, 128)
    room = {name: pltpu.VMEM(arg.shape, arg.dtype) for name, arg in zip(INPUTS, args)}
    shapes = {
        "own": (320, 128),
        "swapped": (5, 8, 8, 128),
        "segments": (16, count),
        "packed": (group, 16, CAP),
        "bundle": (group, 16, CAP),
        "halo_out": (FIRST_ROWS, 128),
        "halo_in": (FIRST_ROWS, 128),
        "halo_out_next": (NEXT_ROWS, 128),
        "halo_in_next": (NEXT_ROWS, 128),
        "mine": (8, count),
        "mine_next": (8, count),
        "slaves_out": parts,
        "slaves_in": parts,
        "masters_out": parts,
        "masters_in": parts,
        "slaves_out_next": parts,
        "slaves_in_next": parts,
        "masters_out_next": parts,
        "masters_in_next": parts,
        "kept": (576, 128),
        "fields": (384, 128),
        "last": (192, 128),
        "wide_mod": (WIDE, 128),
        "wide_mod_up": (WIDE, 128),
        "mass_wide": (1, 4, WIDE, 128),
        "wide": field,
        "wide_up": (3, 3, WIDE, 128),
        "wide_mid": (3, WIDE, 128),
        "out": field,
        "total": (192, 256),
        "pulls": (8, count),
        "tile": (8, 128),
        "middle": (8, 128),
        "across": (extents[0], 8, 128),
        "along": (group, 8, 128),
    }
    room.update({name: pltpu.VMEM(shape, F32) for name, shape in shapes.items()})
    room["places"] = pltpu.VMEM((CAP, count), BF16)
    room["loads"] = dma((len(INPUTS),))
    for name in ("halo", "halo_next"):
        room[name + "_sends"] = room[name + "_receives"] = dma((len(FIRST_PLAN),))
    for name in ("packed", "slaves", "masters", "slaves_next", "masters_next", "sum_along"):
        room[name + "_sends"] = room[name + "_receives"] = dma((group,))
    room["sum_across_sends"] = room["sum_across_receives"] = dma((extents[0],))
    return room


class Refs:
    def __init__(self, names, refs):
        self.__dict__.update(zip(names, refs))


def whole_kernel(extents, names, *refs):
    inputs, (adjoint, residual) = refs[: len(INPUTS)], refs[len(INPUTS) : len(INPUTS) + 2]
    r = Refs(names, refs[len(INPUTS) + 2 :])
    wide, group = extents
    gx, gy = lax.axis_index("gx"), lax.axis_index("gy")
    loads = [
        pltpu.make_async_copy(ref, getattr(r, name), r.loads.at[k])
        for k, (name, ref) in enumerate(zip(INPUTS, inputs))
    ]
    for load in loads:
        load.start()

    def beside(dx, dy):
        return lax.rem(gx + dx + wide, wide), lax.rem(gy + dy + group, group)

    barrier = pltpu.get_barrier_semaphore()
    peers = [(0, k) for k in range(1, group)] + [(k, 0) for k in range(1, wide)]
    peers += [(dx, dy) for dx, dy, _, _, _ in FIRST_PLAN if dx and dy]
    for dx, dy in peers:
        pl.semaphore_signal(barrier, inc=1, device_id=beside(dx, dy), device_id_type=MESH)

    def send(source, target, kind, k, device):
        copy = pltpu.make_async_remote_copy(
            src_ref=source,
            dst_ref=target,
            send_sem=getattr(r, kind + "_sends").at[k],
            recv_sem=getattr(r, kind + "_receives").at[k],
            device_id=device,
            device_id_type=MESH,
        )
        copy.start()
        return copy

    def send_halo(plan, source, target, kind):
        return [
            send(source.at[pl.ds(at, rows)], target.at[pl.ds(at, rows)], kind, k, beside(dx, dy))
            for k, (dx, dy, at, rows, _) in enumerate(plan)
        ]

    def send_blocks(source, target, kind):
        copies = []
        for k in range(1, group):
            device = beside(0, k)
            copies.append(send(source.at[device[1]], target.at[gy], kind, k, device))
        target[gy] = source[gy]
        return copies

    def receive(copies):
        for copy in copies:
            copy.wait_recv()

    for load in loads[:3]:
        load.wait()
    lay_out(r.seed, r.modulus, r.mass, r.own, r.swapped)
    pack_halo(FIRST_PLAN, r.own, r.halo_out)
    pl.semaphore_wait(barrier, len(peers))
    halo = send_halo(FIRST_PLAN, r.halo_out, r.halo_in, "halo")
    for load in loads[3:]:
        load.wait()
    place_segments(
        group,
        r.pair,
        r.slave_nodes,
        r.slave_weights,
        r.master_nodes,
        r.master_weights,
        r.penalty,
        r.packed,
        r.segments,
        r.places,
    )
    bundles = send_blocks(r.packed, r.bundle, "packed")

    r.wide[...] = jnp.zeros_like(r.wide)
    r.mass_wide[...] = jnp.zeros_like(r.mass_wide)
    r.wide_mod[...] = jnp.zeros_like(r.wide_mod)
    for i in range(3):
        widen_own(r.own, i, r.wide, i)
    widen_own(r.own, 3, r.mass_wide, 0)
    for x in range(4):
        r.wide_mod[pl.ds(8 * (x + 2) + 2, 4), :] = r.own[pl.ds(4 * 64 + 4 * x, 4), :]

    def store(array, parity, start, count, stride, value):
        at = rows_of(start, count, stride)
        if array < 3:
            r.wide[array, parity, at, :] = value
        elif array == 3:
            r.mass_wide[0, parity, at, :] = value
        else:
            r.wide_mod[at, :] = value

    receive(halo)
    unpack_halo(FIRST_PLAN, extents, r.halo_in, store)
    r.wide_mod_up[...] = shift_down(r.wide_mod[...])
    diagonal_into(r.out, r.wide_mod, r.wide_mod_up)
    for i in range(3):
        for parity in range(4):
            mass = r.mass_wide[0, parity]
            inverse = jnp.where(mass > 0.0, 1.0 / (r.out[i, parity] + mass), 0.0)
            r.out[i, parity] = inverse
            r.wide[i, parity] = r.wide[i, parity] * inverse
        narrow(r.wide, i, r.kept, i)
        narrow(r.out, i, r.kept, 3 + i)
    table = table_of(r.kept[0:192, :])
    gather_slaves(table, r.segments, r.mine, r.slaves_out, r.places, group)
    slaves = send_blocks(r.slaves_out, r.slaves_in, "slaves")
    receive(bundles)
    gather_masters(table, r.bundle, r.masters_out, group)
    masters = send_blocks(r.masters_out, r.masters_in, "masters")

    def stiffness():
        lift(r.wide, r.wide_up, r.wide_mid)
        stiffness_into(r.out, r.wide, r.wide_up, r.wide_mid, r.wide_mod, r.wide_mod_up)

    stiffness()
    for i in range(3):
        narrow(r.out, i, r.kept, 6 + i)
        at = pl.ds(64 * (6 + i), 64)
        r.kept[at, :] += r.own[pl.ds(192, 64), :] * r.kept[pl.ds(64 * i, 64), :]

    receive(slaves)
    r.total[...] = jnp.zeros_like(r.total)
    scatter_masters(r.total, r.bundle, r.masters_out, r.slaves_in, 0, group)
    receive(masters)
    pull_slaves(r.segments, r.mine, r.masters_in, r.places, r.pulls, group)
    scatter_slaves(r.total, r.segments, r.pulls)
    applied = r.kept[384:576, :] + total_rows(r.total)
    scaled = applied * r.kept[192:384, :]
    r.fields[0:192, :] = scaled
    r.fields[192:384, :] = applied
    pack_halo(NEXT_PLAN, r.fields, r.halo_out_next)
    halo_next = send_halo(NEXT_PLAN, r.halo_out_next, r.halo_in_next, "halo_next")
    table = table_of(scaled)
    gather_slaves(table, r.segments, r.mine_next, r.slaves_out_next, r.places, group)
    slaves_next = send_blocks(r.slaves_out_next, r.slaves_in_next, "slaves_next")
    gather_masters(table, r.bundle, r.masters_out_next, group)
    masters_next = send_blocks(r.masters_out_next, r.masters_in_next, "masters_next")

    r.wide[...] = jnp.zeros_like(r.wide)
    for i in range(3):
        widen_own(r.fields, i, r.wide, i)

    def store_next(array, parity, start, count, stride, value):
        r.wide[array, parity, rows_of(start, count, stride), :] = value

    receive(halo_next)
    unpack_halo(NEXT_PLAN, extents, r.halo_in_next, store_next)
    stiffness()
    for i in range(3):
        narrow(r.out, i, r.last, i)
    seed, direction = r.own[0:192, :], r.kept[0:192, :]
    scaled, applied = r.fields[0:192, :], r.fields[192:384, :]
    mass = r.own[192:256, :]
    smooth = r.last[...] + jnp.concatenate([mass, mass, mass], axis=0) * scaled
    r.last[...] = smooth
    r.tile[0:1, :] = inner(seed, direction)
    r.tile[1:2, :] = inner(direction, applied)
    r.tile[2:3, :] = inner(scaled, applied)
    r.tile[4:8, :] = jnp.zeros((4, 128), F32)

    def masters_from(first, last):
        scatter_masters(r.total, r.bundle, r.masters_out_next, r.slaves_in_next, first, last)

    receive(slaves_next)
    r.total[...] = jnp.zeros_like(r.total)
    masters_from(0, group // 4)
    receive(masters_next)
    gap = pull_slaves(r.segments, r.mine_next, r.masters_in_next, r.places, r.pulls, group)
    pressed = inner(gap, r.pulls[0:3, :])
    energy = inner(scaled, smooth)
    for k in range(pressed.shape[1] // 128):
        energy = energy + pressed[:, 128 * k : 128 * (k + 1)]
    r.tile[3:4, :] = energy
    across = [
        send(r.tile, r.across.at[gx], "sum_across", k, beside(k, 0)) for k in range(1, wide)
    ]
    r.across[gx] = r.tile[...]
    scatter_slaves(r.total, r.segments, r.pulls)
    masters_from(group // 4, group // 2)
    receive(across)
    part = jnp.sum(r.across[...], axis=0)
    r.middle[...] = part
    along = [
        send(r.middle, r.along.at[gy], "sum_along", k, beside(0, k)) for k in range(1, group)
    ]
    r.along[gy] = part
    masters_from(group // 2, group)
    again = r.last[...] + total_rows(r.total)
    receive(along)
    totals = jnp.sum(jnp.sum(r.along[...], axis=0), axis=1, keepdims=True)
    first, second, third, fourth = (totals[k : k + 1] for k in range(4))
    step = first / second
    later = step * step * third - first
    grown = 1.0 + later / first
    curved = grown * grown * second - 2.0 * step * grown * third + step * step * fourth
    step_next = later / curved
    forward = step + step_next * grown
    aside = step_next * step
    adjoint[...] = forward * direction - aside * scaled
    residual[...] = seed - forward * applied + aside * again
    sends = halo + bundles + slaves + masters + halo_next + slaves_next + masters_next
    for copy in sends + across + along:
        copy.wait_send()


def finish_kernel(found, left, adjoint, residual):
    for source, ref in ((found, adjoint), (left, residual)):
        value = reorder(source[...], False)
        for i in range(3):
            for x in range(8):
                for py in range(2):
                    row = i * 64 + (x % 2 * 2 + py) * 16 + x // 2 * 4
                    ref[i, x, pl.ds(py, 4, stride=2), :] = value[row : row + 4]


def shards(
    seed_grad,
    modulus,
    lumped_mass,
    pair_dest,
    slave_nodes,
    slave_weights,
    master_nodes,
    master_weights,
    penalty,
):
    extents = (lax.axis_size("gx"), lax.axis_size("gy"))
    count = penalty.shape[0]
    args = (
        seed_grad,
        modulus,
        lumped_mass,
        pair_dest.reshape(1, count),
        slave_nodes,
        slave_weights,
        master_nodes,
        master_weights,
        penalty.reshape(1, count),
    )
    scratch = scratch_of(extents, args)
    own = jax.ShapeDtypeStruct((192, 128), F32)
    found, left = pl.pallas_call(
        functools.partial(whole_kernel, extents, tuple(scratch)),
        out_shape=[own, own],
        in_specs=[pl.BlockSpec(memory_space=pl.ANY)] * len(args),
        out_specs=[VMEM, VMEM],
        scratch_shapes=list(scratch.values()),
        compiler_params=pltpu.CompilerParams(
            collective_id=1, has_side_effects=True, vmem_limit_bytes=LIMIT
        ),
        name="conjugate_gradients",
    )(*args)
    field = jax.ShapeDtypeStruct(seed_grad.shape, F32)
    return tuple(
        pl.pallas_call(
            finish_kernel,
            out_shape=[field, field],
            in_specs=[VMEM, VMEM],
            out_specs=[VMEM, VMEM],
            compiler_params=pltpu.CompilerParams(vmem_limit_bytes=LIMIT),
            name="finish",
        )(found, left)
    )


def solution(mesh):
    placed = (
        P(None, "gx", "gy", None),
        P("gx", "gy", None),
        P("gx", "gy", None),
        P(("gx", "gy"), None),
        P(None, ("gx", "gy")),
        P(None, ("gx", "gy")),
        P(None, ("gx", "gy")),
        P(None, ("gx", "gy")),
        P(("gx", "gy")),
    )
    return jax.shard_map(
        shards,
        mesh=mesh,
        in_specs=placed,
        out_specs=(P(None, "gx", "gy", None), P(None, "gx", "gy", None)),
        check_vma=False,
    )
```

time: 115 us -> 48 us (0.42)
  Pallas kernels: 106 us -> 47.2 us
  local copies, waits for them, and re-layouts: 7.91 us -> 0 us
    pallas_call x9 -> x2, Pallas kernels: 106 us -> 47.2 us  [the longest x1 45.4 us: shards(): pl.pallas_call(functools.partial(whole_kernel, extents, tuple(scratch)),...]
    unnamed x22 -> x0, local copies, waits for them, and re-layouts: 7.91 us -> none
where the time goes in v2:
time: 48 us; the launch traced here: 47.8 us
  Pallas kernels  47.2 us (98%)
  between operations  0.64 us (1%)
    pallas_call x1, Pallas kernels, shards(): pl.pallas_call(functools.partial(whole_kernel, extents, tuple(scratch)),...  45.4 us
    pallas_call x1, Pallas kernels, shards(): pl.pallas_call(finish_kernel, out_shape=[field, field], in_specs=[VMEM, V...  1.82 us

profile of v2, /device:TPU:1, one launch (start us, length us, event | category | flops | bytes accessed | tf_op | source)
XLA Modules:
  0.0 47.8 jit_solution(11881111919615576145)
XLA Ops:
  0.6 45.4 %conjugate_gradients.1 = (f32[192,128]{1,0:T(8,128)}, f32[192,128]{1,0:T(8,128)}) custom-call(f32[3,8,8,128]{3,2,1,0:T(8,128)} %refs_0_.1, f32[8,8,128]{2,1,0:T(8,128)} %refs_1_.1, f32[8,8,128]{2,1,0:T(8,128)} %refs_2_.1, s32[1,1024]{1,0:T(1,128)} %bitcast.2, s32[4,1024]{1,0:T(4,128)} %refs_4_.1, f32[4,1024]{1,0:T(4,128)} %refs_5_.1, s32[4,1024]{1,0:T(4,128)} %refs_6_.1, ...), custom_call_target="tpu_custom_call" | custom-call | tf_op jit(solution)/shard_map/conjugate_gradients/pallas_call | solution.py:923
  46.0 1.8 %finish.1 = (f32[3,8,8,128]{3,2,1,0:T(8,128)}, f32[3,8,8,128]{3,2,1,0:T(8,128)}) custom-call(f32[192,128]{1,0:T(8,128)} %get-tuple-element.4.found, f32[192,128]{1,0:T(8,128)} %get-tuple-element.5.left), custom_call_target="tpu_custom_call" | custom-call | tf_op jit(solution)/shard_map/finish/pallas_call | solution.py:936

commit v3 on v2

--- a/solution.py
+++ b/solution.py
@@ -288,7 +288,7 @@
         wide_mid[i] = pltpu.roll(wide[i, 0], 64, 1)
 
 
-def halo_plan(fields, with_modulus):
+def halo_plan(fields, modulus=None):
     plan, first = [], 0
     for dx in (-1, 0, 1):
         for dy in (-1, 0, 1):
@@ -318,17 +318,18 @@
                     every if dx == 0 else places(dx, True),
                     every if dy == 0 else places(dy, True),
                 )
-            if with_modulus:
+            if modulus is not None:
                 deep = {1: [(0, 3, 1), (0, 2, 0)], -1: [(0, 0, 6), (0, 1, 7)], 0: every[:1]}
-                strips(fields, deep[dx], deep[dy])
+                strips(modulus, deep[dx], deep[dy])
             rows = sum(piece[3] for piece in pieces)
             plan.append((dx, dy, first, -(-rows // 8) * 8, pieces))
             first += plan[-1][3]
     return plan, first
 
 
-FIRST_PLAN, FIRST_ROWS = halo_plan(4, True)
-NEXT_PLAN, NEXT_ROWS = halo_plan(3, False)
+MODULUS_PLAN, MODULUS_ROWS = halo_plan(0, 4)
+FIRST_PLAN, FIRST_ROWS = halo_plan(4)
+NEXT_PLAN, NEXT_ROWS = halo_plan(3)
 
 
 def rows_of(start, count, stride):
@@ -478,29 +479,28 @@
         [jnp.where(target == t, 1.0, 0.0).astype(BF16) * both for t in range(group)], axis=0
     )
     placed = dot(left, places[...], True).reshape(group, 16, CAP)
-    theirs[...] = placed[:, 0:8] + placed[:, 8:16]
-
-
-def gather_masters(table, bundle, theirs, group):
-    theirs[...] = jnp.zeros_like(theirs)
-
-    def master(source):
+    theirs[...] = placed[:, 0:4] + placed[:, 8:12]
+
+
+def gather_masters(table, bundle, theirs, group, me, first, last):
+    def master(k):
+        source = lax.rem(me + k, group)
         theirs[source, 0:3, :] = gather_block(table, bundle[source])
 
-    each(0, group, master, 8)
+    each(first, last, master, 8)
 
 
 def pull_slaves(segments, mine, returned, places, pulls, group):
-    head, tail = in_two(returned[...].reshape(group * 8, CAP))
+    nothing = jnp.zeros((4, CAP), F32)
+    slots = jnp.concatenate([v for t in range(group) for v in (returned[t], nothing)], axis=0)
+    head, tail = in_two(slots)
     found = dot(
         jnp.concatenate([head, tail], axis=1),
         jnp.concatenate([places[...], places[...]], axis=0),
     )
     target = segments[5:6, :]
     back = sum(jnp.where(target == t, 1.0, 0.0) * found[8 * t : 8 * (t + 1)] for t in range(group))
-    gap = mine[0:3, :] - back[0:3, :]
-    pulls[0:3, :] = segments[4:5, :] * gap
-    return gap
+    pulls[0:3, :] = segments[4:5, :] * (mine[0:3, :] - back[0:3, :])
 
 
 def scatter_slaves(total, segments, pulls):
@@ -538,11 +538,12 @@
     )
 
 
-def lay_out(seed, modulus, mass, own, swapped):
-    values = [seed[...].reshape(192, 128), mass[...].reshape(64, 128)]
-    values.append(modulus[...].reshape(64, 128))
-    swapped[...] = reorder(jnp.concatenate(values, axis=0), True).reshape(5, 8, 8, 128)
-    for array in range(5):
+def lay_out(fields, first, own, swapped):
+    values = [field[...].reshape(-1, 128) for field in fields]
+    value = reorder(values[0] if len(values) == 1 else jnp.concatenate(values, axis=0), True)
+    count = value.shape[0] // 64
+    swapped[pl.ds(first, count)] = value.reshape(count, 8, 8, 128)
+    for array in range(first, first + count):
         for x in range(8):
             for py in range(2):
                 row = array * 64 + (x % 2 * 2 + py) * 16 + x // 2 * 4
@@ -622,9 +623,23 @@
 )
 
 
+KINDS = (
+    "modulus",
+    "halo",
+    "packed",
+    "slaves",
+    "masters",
+    "halo_next",
+    "slaves_next",
+    "masters_next",
+    "across",
+    "along",
+)
+
+
 def scratch_of(extents, args):
     group, count = extents[1], args[-1].shape[-1]
-    dma, parts, field = pltpu.SemaphoreType.DMA, (group, 8, CAP), (3, 4, WIDE, 128)
+    dma, parts, field = pltpu.SemaphoreType.DMA, (group, 4, CAP), (3, 4, WIDE, 128)
     room = {name: pltpu.VMEM(arg.shape, arg.dtype) for name, arg in zip(INPUTS, args)}
     shapes = {
         "own": (320, 128),
@@ -632,6 +647,8 @@
         "segments": (16, count),
         "packed": (group, 16, CAP),
         "bundle": (group, 16, CAP),
+        "modulus_out": (MODULUS_ROWS, 128),
+        "modulus_in": (MODULUS_ROWS, 128),
         "halo_out": (FIRST_ROWS, 128),
         "halo_in": (FIRST_ROWS, 128),
         "halo_out_next": (NEXT_ROWS, 128),
@@ -666,11 +683,8 @@
     room.update({name: pltpu.VMEM(shape, F32) for name, shape in shapes.items()})
     room["places"] = pltpu.VMEM((CAP, count), BF16)
     room["loads"] = dma((len(INPUTS),))
-    for name in ("halo", "halo_next"):
-        room[name + "_sends"] = room[name + "_receives"] = dma((len(FIRST_PLAN),))
-    for name in ("packed", "slaves", "masters", "slaves_next", "masters_next", "sum_along"):
-        room[name + "_sends"] = room[name + "_receives"] = dma((group,))
-    room["sum_across_sends"] = room["sum_across_receives"] = dma((extents[0],))
+    room["sends"] = dma((len(KINDS),))
+    room["receives"] = dma((len(KINDS),))
     return room
 
 
@@ -684,60 +698,77 @@
     r = Refs(names, refs[len(INPUTS) + 2 :])
     wide, group = extents
     gx, gy = lax.axis_index("gx"), lax.axis_index("gy")
-    loads = [
-        pltpu.make_async_copy(ref, getattr(r, name), r.loads.at[k])
+    loads = {
+        name: pltpu.make_async_copy(ref, getattr(r, name), r.loads.at[k])
         for k, (name, ref) in enumerate(zip(INPUTS, inputs))
-    ]
-    for load in loads:
-        load.start()
+    }
+    for name in sorted(loads, key=lambda name: name != "modulus"):
+        loads[name].start()
 
     def beside(dx, dy):
         return lax.rem(gx + dx + wide, wide), lax.rem(gy + dy + group, group)
 
     barrier = pltpu.get_barrier_semaphore()
-    peers = [(0, k) for k in range(1, group)] + [(k, 0) for k in range(1, wide)]
-    peers += [(dx, dy) for dx, dy, _, _, _ in FIRST_PLAN if dx and dy]
+    peers = [(dx, dy) for dx, dy, _, _, _ in FIRST_PLAN]
+    peers += [(k, 0) for k in range(2, wide - 1)] + [(0, k) for k in range(2, group - 1)]
     for dx, dy in peers:
         pl.semaphore_signal(barrier, inc=1, device_id=beside(dx, dy), device_id_type=MESH)
 
-    def send(source, target, kind, k, device):
-        copy = pltpu.make_async_remote_copy(
+    def copy_of(kind, source, target, device):
+        k = KINDS.index(kind)
+        return pltpu.make_async_remote_copy(
             src_ref=source,
             dst_ref=target,
-            send_sem=getattr(r, kind + "_sends").at[k],
-            recv_sem=getattr(r, kind + "_receives").at[k],
+            send_sem=r.sends.at[k],
+            recv_sem=r.receives.at[k],
             device_id=device,
             device_id_type=MESH,
         )
-        copy.start()
-        return copy
+
+    def all_of(kind, buffer, count=None):
+        part = buffer if count is None else buffer.at[pl.ds(0, count)]
+        return copy_of(kind, part, part, beside(0, 1))
+
+    whole = {
+        "modulus": all_of("modulus", r.modulus_in),
+        "halo": all_of("halo", r.halo_in),
+        "packed": all_of("packed", r.bundle, group - 1),
+        "slaves": all_of("slaves", r.slaves_in, group - 1),
+        "masters": all_of("masters", r.masters_in, group - 1),
+        "halo_next": all_of("halo_next", r.halo_in_next),
+        "slaves_next": all_of("slaves_next", r.slaves_in_next, group - 1),
+        "masters_next": all_of("masters_next", r.masters_in_next, group - 1),
+        "across": all_of("across", r.across, wide - 1),
+        "along": all_of("along", r.along, group - 1),
+    }
+
+    def receive(kind):
+        whole[kind].wait_recv()
 
     def send_halo(plan, source, target, kind):
-        return [
-            send(source.at[pl.ds(at, rows)], target.at[pl.ds(at, rows)], kind, k, beside(dx, dy))
-            for k, (dx, dy, at, rows, _) in enumerate(plan)
-        ]
-
-    def send_blocks(source, target, kind):
-        copies = []
-        for k in range(1, group):
+        for dx, dy, at, rows, _ in plan:
+            part = pl.ds(at, rows)
+            copy_of(kind, source.at[part], target.at[part], beside(dx, dy)).start()
+
+    def send_blocks(source, target, kind, first=1, last=group):
+        for k in range(first, last):
             device = beside(0, k)
-            copies.append(send(source.at[device[1]], target.at[gy], kind, k, device))
-        target[gy] = source[gy]
-        return copies
-
-    def receive(copies):
-        for copy in copies:
-            copy.wait_recv()
-
-    for load in loads[:3]:
-        load.wait()
-    lay_out(r.seed, r.modulus, r.mass, r.own, r.swapped)
+            copy_of(kind, source.at[device[1]], target.at[gy], device).start()
+        if first == 1:
+            target[gy] = source[gy]
+
+    loads["modulus"].wait()
+    lay_out([r.modulus], 4, r.own, r.swapped)
+    pack_halo(MODULUS_PLAN, r.own, r.modulus_out)
+    pl.semaphore_wait(barrier, len(peers))
+    send_halo(MODULUS_PLAN, r.modulus_out, r.modulus_in, "modulus")
+    loads["seed"].wait()
+    loads["mass"].wait()
+    lay_out([r.seed, r.mass], 0, r.own, r.swapped)
     pack_halo(FIRST_PLAN, r.own, r.halo_out)
-    pl.semaphore_wait(barrier, len(peers))
-    halo = send_halo(FIRST_PLAN, r.halo_out, r.halo_in, "halo")
-    for load in loads[3:]:
-        load.wait()
+    send_halo(FIRST_PLAN, r.halo_out, r.halo_in, "halo")
+    for name in INPUTS[3:]:
+        loads[name].wait()
     place_segments(
         group,
         r.pair,
@@ -750,7 +781,7 @@
         r.segments,
         r.places,
     )
-    bundles = send_blocks(r.packed, r.bundle, "packed")
+    send_blocks(r.packed, r.bundle, "packed")
 
     r.wide[...] = jnp.zeros_like(r.wide)
     r.mass_wide[...] = jnp.zeros_like(r.mass_wide)
@@ -760,34 +791,45 @@
     widen_own(r.own, 3, r.mass_wide, 0)
     for x in range(4):
         r.wide_mod[pl.ds(8 * (x + 2) + 2, 4), :] = r.own[pl.ds(4 * 64 + 4 * x, 4), :]
+    for buffer in (r.masters_out, r.masters_out_next):
+        buffer[...] = jnp.zeros_like(buffer)
+
+    def store_modulus(array, parity, start, count, stride, value):
+        r.wide_mod[rows_of(start, count, stride), :] = value
+
+    receive("modulus")
+    unpack_halo(MODULUS_PLAN, extents, r.modulus_in, store_modulus)
+    r.wide_mod_up[...] = shift_down(r.wide_mod[...])
+    diagonal_into(r.out, r.wide_mod, r.wide_mod_up)
+    for i in range(3):
+        narrow(r.out, i, r.kept, 3 + i)
+    mass = r.own[192:256, :]
+    masses = jnp.concatenate([mass, mass, mass], axis=0)
+    r.kept[192:384, :] = 1.0 / (r.kept[192:384, :] + masses)
+    r.kept[0:192, :] = r.own[0:192, :] * r.kept[192:384, :]
+    table = table_of(r.kept[0:192, :])
+    gather_slaves(table, r.segments, r.mine, r.slaves_out, r.places, group)
+    send_blocks(r.slaves_out, r.slaves_in, "slaves")
+    receive("packed")
+    gather_masters(table, r.bundle, r.masters_out, group, gy, 0, group // 2)
+    send_blocks(r.masters_out, r.masters_in, "masters", 1, group // 2)
+    gather_masters(table, r.bundle, r.masters_out, group, gy, group // 2, group)
+    send_blocks(r.masters_out, r.masters_in, "masters", group // 2, group)
 
     def store(array, parity, start, count, stride, value):
         at = rows_of(start, count, stride)
         if array < 3:
             r.wide[array, parity, at, :] = value
-        elif array == 3:
+        else:
             r.mass_wide[0, parity, at, :] = value
-        else:
-            r.wide_mod[at, :] = value
-
-    receive(halo)
+
+    receive("halo")
     unpack_halo(FIRST_PLAN, extents, r.halo_in, store)
-    r.wide_mod_up[...] = shift_down(r.wide_mod[...])
-    diagonal_into(r.out, r.wide_mod, r.wide_mod_up)
     for i in range(3):
         for parity in range(4):
-            mass = r.mass_wide[0, parity]
-            inverse = jnp.where(mass > 0.0, 1.0 / (r.out[i, parity] + mass), 0.0)
-            r.out[i, parity] = inverse
+            wide_mass = r.mass_wide[0, parity]
+            inverse = jnp.where(wide_mass > 0.0, 1.0 / (r.out[i, parity] + wide_mass), 0.0)
             r.wide[i, parity] = r.wide[i, parity] * inverse
-        narrow(r.wide, i, r.kept, i)
-        narrow(r.out, i, r.kept, 3 + i)
-    table = table_of(r.kept[0:192, :])
-    gather_slaves(table, r.segments, r.mine, r.slaves_out, r.places, group)
-    slaves = send_blocks(r.slaves_out, r.slaves_in, "slaves")
-    receive(bundles)
-    gather_masters(table, r.bundle, r.masters_out, group)
-    masters = send_blocks(r.masters_out, r.masters_in, "masters")
 
     def stiffness():
         lift(r.wide, r.wide_up, r.wide_mid)
@@ -796,13 +838,12 @@
     stiffness()
     for i in range(3):
         narrow(r.out, i, r.kept, 6 + i)
-        at = pl.ds(64 * (6 + i), 64)
-        r.kept[at, :] += r.own[pl.ds(192, 64), :] * r.kept[pl.ds(64 * i, 64), :]
-
-    receive(slaves)
+    r.kept[384:576, :] += masses * r.kept[0:192, :]
+
+    receive("slaves")
     r.total[...] = jnp.zeros_like(r.total)
     scatter_masters(r.total, r.bundle, r.masters_out, r.slaves_in, 0, group)
-    receive(masters)
+    receive("masters")
     pull_slaves(r.segments, r.mine, r.masters_in, r.places, r.pulls, group)
     scatter_slaves(r.total, r.segments, r.pulls)
     applied = r.kept[384:576, :] + total_rows(r.total)
@@ -810,12 +851,14 @@
     r.fields[0:192, :] = scaled
     r.fields[192:384, :] = applied
     pack_halo(NEXT_PLAN, r.fields, r.halo_out_next)
-    halo_next = send_halo(NEXT_PLAN, r.halo_out_next, r.halo_in_next, "halo_next")
+    send_halo(NEXT_PLAN, r.halo_out_next, r.halo_in_next, "halo_next")
     table = table_of(scaled)
     gather_slaves(table, r.segments, r.mine_next, r.slaves_out_next, r.places, group)
-    slaves_next = send_blocks(r.slaves_out_next, r.slaves_in_next, "slaves_next")
-    gather_masters(table, r.bundle, r.masters_out_next, group)
-    masters_next = send_blocks(r.masters_out_next, r.masters_in_next, "masters_next")
+    send_blocks(r.slaves_out_next, r.slaves_in_next, "slaves_next")
+    gather_masters(table, r.bundle, r.masters_out_next, group, gy, 0, group // 2)
+    send_blocks(r.masters_out_next, r.masters_in_next, "masters_next", 1, group // 2)
+    gather_masters(table, r.bundle, r.masters_out_next, group, gy, group // 2, group)
+    send_blocks(r.masters_out_next, r.masters_in_next, "masters_next", group // 2, group)
 
     r.wide[...] = jnp.zeros_like(r.wide)
     for i in range(3):
@@ -824,50 +867,50 @@
     def store_next(array, parity, start, count, stride, value):
         r.wide[array, parity, rows_of(start, count, stride), :] = value
 
-    receive(halo_next)
+    receive("halo_next")
     unpack_halo(NEXT_PLAN, extents, r.halo_in_next, store_next)
     stiffness()
     for i in range(3):
         narrow(r.out, i, r.last, i)
     seed, direction = r.own[0:192, :], r.kept[0:192, :]
     scaled, applied = r.fields[0:192, :], r.fields[192:384, :]
-    mass = r.own[192:256, :]
-    smooth = r.last[...] + jnp.concatenate([mass, mass, mass], axis=0) * scaled
+    smooth = r.last[...] + masses * scaled
     r.last[...] = smooth
     r.tile[0:1, :] = inner(seed, direction)
     r.tile[1:2, :] = inner(direction, applied)
     r.tile[2:3, :] = inner(scaled, applied)
     r.tile[4:8, :] = jnp.zeros((4, 128), F32)
+    receive("slaves_next")
+    pressed = jnp.zeros((3, CAP), F32)
+    for source in range(group):
+        gap = r.masters_out_next[source, 0:3, :] - r.slaves_in_next[source, 0:3, :]
+        pressed = pressed + r.bundle[source, 4:5, :] * gap * gap
+    pressed = jnp.sum(pressed, axis=0, keepdims=True)
+    energy = inner(scaled, smooth)
+    for k in range(CAP // 128):
+        energy = energy + pressed[:, 128 * k : 128 * (k + 1)]
+    r.tile[3:4, :] = energy
+    for k in range(1, wide):
+        copy_of("across", r.tile, r.across.at[gx], beside(k, 0)).start()
+    r.across[gx] = r.tile[...]
 
     def masters_from(first, last):
         scatter_masters(r.total, r.bundle, r.masters_out_next, r.slaves_in_next, first, last)
 
-    receive(slaves_next)
     r.total[...] = jnp.zeros_like(r.total)
-    masters_from(0, group // 4)
-    receive(masters_next)
-    gap = pull_slaves(r.segments, r.mine_next, r.masters_in_next, r.places, r.pulls, group)
-    pressed = inner(gap, r.pulls[0:3, :])
-    energy = inner(scaled, smooth)
-    for k in range(pressed.shape[1] // 128):
-        energy = energy + pressed[:, 128 * k : 128 * (k + 1)]
-    r.tile[3:4, :] = energy
-    across = [
-        send(r.tile, r.across.at[gx], "sum_across", k, beside(k, 0)) for k in range(1, wide)
-    ]
-    r.across[gx] = r.tile[...]
-    scatter_slaves(r.total, r.segments, r.pulls)
-    masters_from(group // 4, group // 2)
-    receive(across)
+    masters_from(0, group // 2)
+    receive("across")
     part = jnp.sum(r.across[...], axis=0)
     r.middle[...] = part
-    along = [
-        send(r.middle, r.along.at[gy], "sum_along", k, beside(0, k)) for k in range(1, group)
-    ]
+    for k in range(1, group):
+        copy_of("along", r.middle, r.along.at[gy], beside(0, k)).start()
     r.along[gy] = part
     masters_from(group // 2, group)
+    receive("masters_next")
+    pull_slaves(r.segments, r.mine_next, r.masters_in_next, r.places, r.pulls, group)
+    scatter_slaves(r.total, r.segments, r.pulls)
     again = r.last[...] + total_rows(r.total)
-    receive(along)
+    receive("along")
     totals = jnp.sum(jnp.sum(r.along[...], axis=0), axis=1, keepdims=True)
     first, second, third, fourth = (totals[k : k + 1] for k in range(4))
     step = first / second
@@ -879,9 +922,8 @@
     aside = step_next * step
     adjoint[...] = forward * direction - aside * scaled
     residual[...] = seed - forward * applied + aside * again
-    sends = halo + bundles + slaves + masters + halo_next + slaves_next + masters_next
-    for copy in sends + across + along:
-        copy.wait_send()
+    for kind in KINDS:
+        whole[kind].wait_send()
 
 
 def finish_kernel(found, left, adjoint, residual):

time: 48 us -> 42.5 us (0.89)
  Pallas kernels: 47.2 us -> 41.7 us
    pallas_call x1, Pallas kernels: 45.4 us -> 39.9 us  [shards(): pl.pallas_call(functools.partial(whole_kernel, extents, tuple(scratch)),...]
where the time goes in v3:
time: 42.5 us; the launch traced here: 42.3 us
  Pallas kernels  41.7 us (98%)
  between operations  0.64 us (2%)
    pallas_call x1, Pallas kernels, shards(): pl.pallas_call(functools.partial(whole_kernel, extents, tuple(scratch)),...  39.9 us
    pallas_call x1, Pallas kernels, shards(): pl.pallas_call(finish_kernel, out_shape=[field, field], in_specs=[VMEM, V...  1.82 us

profile of v3, /device:TPU:1, one launch (start us, length us, event | category | flops | bytes accessed | tf_op | source)
XLA Modules:
  0.0 42.3 jit_solution(4177143275476701646)
XLA Ops:
  0.6 39.9 %conjugate_gradients.1 = (f32[192,128]{1,0:T(8,128)}, f32[192,128]{1,0:T(8,128)}) custom-call(f32[3,8,8,128]{3,2,1,0:T(8,128)} %refs_0_.1, f32[8,8,128]{2,1,0:T(8,128)} %refs_1_.1, f32[8,8,128]{2,1,0:T(8,128)} %refs_2_.1, s32[1,1024]{1,0:T(1,128)} %bitcast.2, s32[4,1024]{1,0:T(4,128)} %refs_4_.1, f32[4,1024]{1,0:T(4,128)} %refs_5_.1, s32[4,1024]{1,0:T(4,128)} %refs_6_.1, ...), custom_call_target="tpu_custom_call" | custom-call | tf_op jit(solution)/shard_map/conjugate_gradients/pallas_call | solution.py:965
  40.5 1.8 %finish.1 = (f32[3,8,8,128]{3,2,1,0:T(8,128)}, f32[3,8,8,128]{3,2,1,0:T(8,128)}) custom-call(f32[192,128]{1,0:T(8,128)} %get-tuple-element.4.found, f32[192,128]{1,0:T(8,128)} %get-tuple-element.5.left), custom_call_target="tpu_custom_call" | custom-call | tf_op jit(solution)/shard_map/finish/pallas_call | solution.py:978

commit v4 on v3

--- a/solution.py
+++ b/solution.py
@@ -129,6 +129,10 @@
     return total
 
 
+def rows_at(group, shift):
+    return pl.ds(pl.multiple_of(8 * group, 8) + shift, 8)
+
+
 def lanes(rows):
     return lax.broadcasted_iota(jnp.int32, (rows, 128), 1)
 
@@ -148,7 +152,7 @@
     values = []
     for c in range(8):
         ref = wide_mod_up if c & 1 else wide_mod
-        values.append(ref[pl.ds(8 * (group + (c >> 2)) + (c >> 1 & 1), 8), :])
+        values.append(ref[rows_at(group + (c >> 2), c >> 1 & 1), :])
     inside = lanes(8) < 64
     return split_sums([jnp.where(inside, value, 0.0) for value in values])
 
@@ -160,25 +164,28 @@
 
 
 def add_rows(ref, index, row, value):
-    ref[index + (pl.ds(row, 8), slice(None))] += value
+    ref[index + (row, slice(None))] += value
 
 
 def scatter_forces(out, i, corner, edges, group):
     for xy in range(4):
-        row = 8 * (group + (xy >> 1)) + (xy & 1)
+        row = rows_at(group + (xy >> 1), xy & 1)
         add_rows(out, (i, 0), row, collect(corner[2 * xy], edges[2][xy], corner[2 * xy + 1]))
     for y in range(2):
-        add_rows(out, (i, 2), 8 * group + y, collect(edges[0][2 * y], None, edges[0][2 * y + 1]))
+        add_rows(
+            out, (i, 2), rows_at(group, y), collect(edges[0][2 * y], None, edges[0][2 * y + 1])
+        )
     for x in range(2):
         add_rows(
-            out, (i, 1), 8 * (group + x), collect(edges[1][2 * x], None, edges[1][2 * x + 1])
+            out, (i, 1), rows_at(group + x, 0), collect(edges[1][2 * x], None, edges[1][2 * x + 1])
         )
 
 
 def diagonal_into(out, wide_mod, wide_mod_up):
     corner_diag, edge_diag = element_tables()[3:]
     out[...] = jnp.zeros_like(out)
-    for group in range(7):
+
+    def step(group, carry):
         moduli = corner_moduli(wide_mod, wide_mod_up, group)
         for i in range(3):
             corner = join_sums(
@@ -197,12 +204,16 @@
                 for d in range(3)
             ]
             scatter_forces(out, i, corner, edges, group)
+        return carry
+
+    lax.fori_loop(0, 7, step, 0, unroll=7)
 
 
 def stiffness_into(out, wide, wide_up, wide_mid, wide_mod, wide_mod_up):
     corner_terms, edge_terms, trilinear = element_tables()[:3]
     out[...] = jnp.zeros_like(out)
-    for group in range(1, 6):
+
+    def step(group, carry):
         moduli = corner_moduli(wide_mod, wide_mod_up, group)
         points = join_sums([moduli[t] * np.float32(trilinear[t]) for t in range(8)])
         slopes = []
@@ -210,19 +221,19 @@
             corner = []
             for c in range(8):
                 ref = wide_up if c & 1 else wide
-                corner.append(ref[i, 0, pl.ds(8 * (group + (c >> 2)) + (c >> 1 & 1), 8), :])
+                corner.append(ref[i, 0, rows_at(group + (c >> 2), c >> 1 & 1), :])
             corner = split_sums(corner)
             edges = []
             for d in range(3):
                 values = []
                 for c in range(4):
                     x, y, z = edge_corner(d, c)
-                    row = 8 * (group + (x or 0)) + (y or 0)
+                    row = rows_at(group + (x or 0), y or 0)
                     parity = (2, 1, 0)[d]
                     if d == 2:
-                        values.append(wide_mid[i, pl.ds(row, 8), :])
+                        values.append(wide_mid[i, row, :])
                     else:
-                        values.append((wide_up if z else wide)[i, parity, pl.ds(row, 8), :])
+                        values.append((wide_up if z else wide)[i, parity, row, :])
                 edges.append(split_sums(values))
             slopes.append(
                 [
@@ -279,6 +290,9 @@
                 for d in range(3)
             ]
             scatter_forces(out, i, corner, edges, group)
+        return carry
+
+    lax.fori_loop(1, 6, step, 0, unroll=5)
 
 
 def lift(wide, wide_up, wide_mid):
@@ -400,6 +414,8 @@
 
 
 BLOCK = CAP
+GATHER_UNROLL = 8
+SCATTER_UNROLL = 4
 
 
 def picks_of(lane, extent):
@@ -482,12 +498,12 @@
     theirs[...] = placed[:, 0:4] + placed[:, 8:12]
 
 
-def gather_masters(table, bundle, theirs, group, me, first, last):
+def gather_masters(table, bundle, theirs, group, first, count):
     def master(k):
-        source = lax.rem(me + k, group)
+        source = lax.rem(first + k, group)
         theirs[source, 0:3, :] = gather_block(table, bundle[source])
 
-    each(first, last, master, 8)
+    each(0, count, master, GATHER_UNROLL)
 
 
 def pull_slaves(segments, mine, returned, places, pulls, group):
@@ -511,14 +527,14 @@
     each(0, segments.shape[1] // (2 * BLOCK), slave, 2)
 
 
-def scatter_masters(total, bundle, sent, arrived, first, last):
+def scatter_masters(total, bundle, sent, arrived, first, count):
     def master(k):
-        pair = [2 * k, 2 * k + 1]
+        pair = [first + 2 * k, first + 2 * k + 1]
         block = jnp.concatenate([bundle[source] for source in pair], axis=1)
         gap = [sent[source, 0:3, :] - arrived[source, 0:3, :] for source in pair]
         total[...] += scatter_block(block, block[4:5] * jnp.concatenate(gap, axis=1))
 
-    each(first // 2, last // 2, master, 4)
+    each(0, count // 2, master, SCATTER_UNROLL)
 
 
 def swap_lanes(forth):
@@ -623,18 +639,16 @@
 )
 
 
-KINDS = (
-    "modulus",
-    "halo",
-    "packed",
-    "slaves",
-    "masters",
-    "halo_next",
-    "slaves_next",
-    "masters_next",
-    "across",
-    "along",
-)
+KINDS = {
+    "modulus": 0,
+    "halo": 1,
+    "packed": 2,
+    "slaves": 3,
+    "masters": 5,
+    "halo_next": 7,
+    "across": 8,
+    "along": 9,
+}
 
 
 def scratch_of(extents, args):
@@ -653,19 +667,14 @@
         "halo_in": (FIRST_ROWS, 128),
         "halo_out_next": (NEXT_ROWS, 128),
         "halo_in_next": (NEXT_ROWS, 128),
-        "mine": (8, count),
-        "mine_next": (8, count),
-        "slaves_out": parts,
-        "slaves_in": parts,
-        "masters_out": parts,
-        "masters_in": parts,
-        "slaves_out_next": parts,
-        "slaves_in_next": parts,
-        "masters_out_next": parts,
-        "masters_in_next": parts,
-        "kept": (576, 128),
-        "fields": (384, 128),
-        "last": (192, 128),
+        "mine": (2, 8, count),
+        "slaves_out": (2,) + parts,
+        "slaves_in": (2,) + parts,
+        "masters_out": (2,) + parts,
+        "masters_in": (2,) + parts,
+        "vectors": (2, 192, 128),
+        "applied": (2, 192, 128),
+        "inverse": (192, 128),
         "wide_mod": (WIDE, 128),
         "wide_mod_up": (WIDE, 128),
         "mass_wide": (1, 4, WIDE, 128),
@@ -683,8 +692,8 @@
     room.update({name: pltpu.VMEM(shape, F32) for name, shape in shapes.items()})
     room["places"] = pltpu.VMEM((CAP, count), BF16)
     room["loads"] = dma((len(INPUTS),))
-    room["sends"] = dma((len(KINDS),))
-    room["receives"] = dma((len(KINDS),))
+    room["sends"] = dma((10,))
+    room["receives"] = dma((10,))
     return room
 
 
@@ -714,8 +723,8 @@
     for dx, dy in peers:
         pl.semaphore_signal(barrier, inc=1, device_id=beside(dx, dy), device_id_type=MESH)
 
-    def copy_of(kind, source, target, device):
-        k = KINDS.index(kind)
+    def copy_of(kind, source, target, device, turn=0):
+        k = KINDS[kind] + turn
         return pltpu.make_async_remote_copy(
             src_ref=source,
             dst_ref=target,
@@ -725,37 +734,35 @@
             device_id_type=MESH,
         )
 
-    def all_of(kind, buffer, count=None):
-        part = buffer if count is None else buffer.at[pl.ds(0, count)]
-        return copy_of(kind, part, part, beside(0, 1))
-
-    whole = {
-        "modulus": all_of("modulus", r.modulus_in),
-        "halo": all_of("halo", r.halo_in),
-        "packed": all_of("packed", r.bundle, group - 1),
-        "slaves": all_of("slaves", r.slaves_in, group - 1),
-        "masters": all_of("masters", r.masters_in, group - 1),
-        "halo_next": all_of("halo_next", r.halo_in_next),
-        "slaves_next": all_of("slaves_next", r.slaves_in_next, group - 1),
-        "masters_next": all_of("masters_next", r.masters_in_next, group - 1),
-        "across": all_of("across", r.across, wide - 1),
-        "along": all_of("along", r.along, group - 1),
-    }
-
-    def receive(kind):
-        whole[kind].wait_recv()
+    def all_of(kind, turn=0):
+        buffers = {"modulus": r.modulus_in, "halo": r.halo_in, "halo_next": r.halo_in_next}
+        if kind in buffers:
+            part = buffers[kind]
+        elif kind in ("slaves", "masters"):
+            part = (r.slaves_in if kind == "slaves" else r.masters_in).at[turn]
+            part = part.at[pl.ds(0, group - 1)]
+        elif kind == "across":
+            part = r.across.at[pl.ds(0, wide - 1)]
+        else:
+            part = (r.bundle if kind == "packed" else r.along).at[pl.ds(0, group - 1)]
+        return copy_of(kind, part, part, beside(0, 1), turn)
+
+    def receive(kind, turn=0):
+        all_of(kind, turn).wait_recv()
 
     def send_halo(plan, source, target, kind):
         for dx, dy, at, rows, _ in plan:
             part = pl.ds(at, rows)
             copy_of(kind, source.at[part], target.at[part], beside(dx, dy)).start()
 
-    def send_blocks(source, target, kind, first=1, last=group):
-        for k in range(first, last):
-            device = beside(0, k)
-            copy_of(kind, source.at[device[1]], target.at[gy], device).start()
-        if first == 1:
-            target[gy] = source[gy]
+    def send_block(source, target, kind, k, turn):
+        device = beside(0, k)
+        copy_of(kind, source.at[device[1]], target.at[gy], device, turn).start()
+
+    def send_blocks(source, target, kind, turn=0):
+        for k in range(1, group):
+            send_block(source, target, kind, k, turn)
+        target[gy] = source[gy]
 
     loads["modulus"].wait()
     lay_out([r.modulus], 4, r.own, r.swapped)
@@ -791,8 +798,7 @@
     widen_own(r.own, 3, r.mass_wide, 0)
     for x in range(4):
         r.wide_mod[pl.ds(8 * (x + 2) + 2, 4), :] = r.own[pl.ds(4 * 64 + 4 * x, 4), :]
-    for buffer in (r.masters_out, r.masters_out_next):
-        buffer[...] = jnp.zeros_like(buffer)
+    r.masters_out[...] = jnp.zeros_like(r.masters_out)
 
     def store_modulus(array, parity, start, count, stride, value):
         r.wide_mod[rows_of(start, count, stride), :] = value
@@ -802,19 +808,10 @@
     r.wide_mod_up[...] = shift_down(r.wide_mod[...])
     diagonal_into(r.out, r.wide_mod, r.wide_mod_up)
     for i in range(3):
-        narrow(r.out, i, r.kept, 3 + i)
+        narrow(r.out, i, r.inverse, i)
     mass = r.own[192:256, :]
-    masses = jnp.concatenate([mass, mass, mass], axis=0)
-    r.kept[192:384, :] = 1.0 / (r.kept[192:384, :] + masses)
-    r.kept[0:192, :] = r.own[0:192, :] * r.kept[192:384, :]
-    table = table_of(r.kept[0:192, :])
-    gather_slaves(table, r.segments, r.mine, r.slaves_out, r.places, group)
-    send_blocks(r.slaves_out, r.slaves_in, "slaves")
-    receive("packed")
-    gather_masters(table, r.bundle, r.masters_out, group, gy, 0, group // 2)
-    send_blocks(r.masters_out, r.masters_in, "masters", 1, group // 2)
-    gather_masters(table, r.bundle, r.masters_out, group, gy, group // 2, group)
-    send_blocks(r.masters_out, r.masters_in, "masters", group // 2, group)
+    r.inverse[...] = 1.0 / (r.inverse[...] + jnp.concatenate([mass, mass, mass], axis=0))
+    r.vectors[0] = r.own[0:192, :] * r.inverse[...]
 
     def store(array, parity, start, count, stride, value):
         at = rows_of(start, count, stride)
@@ -823,93 +820,117 @@
         else:
             r.mass_wide[0, parity, at, :] = value
 
-    receive("halo")
-    unpack_halo(FIRST_PLAN, extents, r.halo_in, store)
-    for i in range(3):
-        for parity in range(4):
-            wide_mass = r.mass_wide[0, parity]
-            inverse = jnp.where(wide_mass > 0.0, 1.0 / (r.out[i, parity] + wide_mass), 0.0)
-            r.wide[i, parity] = r.wide[i, parity] * inverse
-
-    def stiffness():
+    def apply(turn, carry):
+        begins, ends = turn == 0, turn == 1
+        mine = r.mine.at[turn]
+        slaves_out, slaves_in = r.slaves_out.at[turn], r.slaves_in.at[turn]
+        masters_out, masters_in = r.masters_out.at[turn], r.masters_in.at[turn]
+        table = table_of(r.vectors[turn])
+        gather_slaves(table, r.segments, mine, slaves_out, r.places, group)
+        send_blocks(slaves_out, slaves_in, "slaves", turn)
+
+        @pl.when(begins)
+        def _segments():
+            receive("packed")
+
+        half = group // 2
+
+        def masters(k, carry):
+            first = half * k
+            gather_masters(table_of(r.vectors[turn]), r.bundle, masters_out, group, gy + first, half)
+
+            @pl.when(k > 0)
+            def _middle():
+                send_block(masters_out, masters_in, "masters", first, turn)
+
+            for j in range(1, half):
+                send_block(masters_out, masters_in, "masters", first + j, turn)
+            return carry
+
+        lax.fori_loop(0, 2, masters, 0)
+        masters_in[gy] = masters_out[gy]
+
+        @pl.when(begins)
+        def _first():
+            receive("halo")
+            unpack_halo(FIRST_PLAN, extents, r.halo_in, store)
+            for i in range(3):
+                for parity in range(4):
+                    wide_mass = r.mass_wide[0, parity]
+                    entry = r.out[i, parity] + wide_mass
+                    inverse = jnp.where(wide_mass > 0.0, 1.0 / entry, 0.0)
+                    r.wide[i, parity] = r.wide[i, parity] * inverse
+
+        @pl.when(ends)
+        def _next():
+            r.wide[...] = jnp.zeros_like(r.wide)
+            for i in range(3):
+                widen_own(r.vectors.at[1], i, r.wide, i)
+            receive("halo_next")
+            unpack_halo(NEXT_PLAN, extents, r.halo_in_next, store)
+
         lift(r.wide, r.wide_up, r.wide_mid)
         stiffness_into(r.out, r.wide, r.wide_up, r.wide_mid, r.wide_mod, r.wide_mod_up)
-
-    stiffness()
-    for i in range(3):
-        narrow(r.out, i, r.kept, 6 + i)
-    r.kept[384:576, :] += masses * r.kept[0:192, :]
-
-    receive("slaves")
-    r.total[...] = jnp.zeros_like(r.total)
-    scatter_masters(r.total, r.bundle, r.masters_out, r.slaves_in, 0, group)
-    receive("masters")
-    pull_slaves(r.segments, r.mine, r.masters_in, r.places, r.pulls, group)
-    scatter_slaves(r.total, r.segments, r.pulls)
-    applied = r.kept[384:576, :] + total_rows(r.total)
-    scaled = applied * r.kept[192:384, :]
-    r.fields[0:192, :] = scaled
-    r.fields[192:384, :] = applied
-    pack_halo(NEXT_PLAN, r.fields, r.halo_out_next)
-    send_halo(NEXT_PLAN, r.halo_out_next, r.halo_in_next, "halo_next")
-    table = table_of(scaled)
-    gather_slaves(table, r.segments, r.mine_next, r.slaves_out_next, r.places, group)
-    send_blocks(r.slaves_out_next, r.slaves_in_next, "slaves_next")
-    gather_masters(table, r.bundle, r.masters_out_next, group, gy, 0, group // 2)
-    send_blocks(r.masters_out_next, r.masters_in_next, "masters_next", 1, group // 2)
-    gather_masters(table, r.bundle, r.masters_out_next, group, gy, group // 2, group)
-    send_blocks(r.masters_out_next, r.masters_in_next, "masters_next", group // 2, group)
-
-    r.wide[...] = jnp.zeros_like(r.wide)
-    for i in range(3):
-        widen_own(r.fields, i, r.wide, i)
-
-    def store_next(array, parity, start, count, stride, value):
-        r.wide[array, parity, rows_of(start, count, stride), :] = value
-
-    receive("halo_next")
-    unpack_halo(NEXT_PLAN, extents, r.halo_in_next, store_next)
-    stiffness()
-    for i in range(3):
-        narrow(r.out, i, r.last, i)
-    seed, direction = r.own[0:192, :], r.kept[0:192, :]
-    scaled, applied = r.fields[0:192, :], r.fields[192:384, :]
-    smooth = r.last[...] + masses * scaled
-    r.last[...] = smooth
-    r.tile[0:1, :] = inner(seed, direction)
-    r.tile[1:2, :] = inner(direction, applied)
-    r.tile[2:3, :] = inner(scaled, applied)
-    r.tile[4:8, :] = jnp.zeros((4, 128), F32)
-    receive("slaves_next")
-    pressed = jnp.zeros((3, CAP), F32)
-    for source in range(group):
-        gap = r.masters_out_next[source, 0:3, :] - r.slaves_in_next[source, 0:3, :]
-        pressed = pressed + r.bundle[source, 4:5, :] * gap * gap
-    pressed = jnp.sum(pressed, axis=0, keepdims=True)
-    energy = inner(scaled, smooth)
-    for k in range(CAP // 128):
-        energy = energy + pressed[:, 128 * k : 128 * (k + 1)]
-    r.tile[3:4, :] = energy
-    for k in range(1, wide):
-        copy_of("across", r.tile, r.across.at[gx], beside(k, 0)).start()
-    r.across[gx] = r.tile[...]
-
-    def masters_from(first, last):
-        scatter_masters(r.total, r.bundle, r.masters_out_next, r.slaves_in_next, first, last)
-
-    r.total[...] = jnp.zeros_like(r.total)
-    masters_from(0, group // 2)
-    receive("across")
-    part = jnp.sum(r.across[...], axis=0)
-    r.middle[...] = part
-    for k in range(1, group):
-        copy_of("along", r.middle, r.along.at[gy], beside(0, k)).start()
-    r.along[gy] = part
-    masters_from(group // 2, group)
-    receive("masters_next")
-    pull_slaves(r.segments, r.mine_next, r.masters_in_next, r.places, r.pulls, group)
-    scatter_slaves(r.total, r.segments, r.pulls)
-    again = r.last[...] + total_rows(r.total)
+        applied = r.applied.at[turn]
+        for i in range(3):
+            narrow(r.out, i, applied, i)
+        mass = r.own[192:256, :]
+        applied[...] += jnp.concatenate([mass, mass, mass], axis=0) * r.vectors[turn]
+        receive("slaves", turn)
+
+        @pl.when(ends)
+        def _sums():
+            scaled = r.vectors[1]
+            r.tile[0:1, :] = inner(r.own[0:192, :], r.vectors[0])
+            r.tile[1:2, :] = inner(r.vectors[0], r.applied[0])
+            r.tile[2:3, :] = inner(scaled, r.applied[0])
+            r.tile[4:8, :] = jnp.zeros((4, 128), F32)
+            pressed = jnp.zeros((3, CAP), F32)
+            for source in range(group):
+                gap = r.masters_out[1, source, 0:3, :] - r.slaves_in[1, source, 0:3, :]
+                pressed = pressed + r.bundle[source, 4:5, :] * gap * gap
+            pressed = jnp.sum(pressed, axis=0, keepdims=True)
+            energy = inner(scaled, r.applied[1])
+            for k in range(CAP // 128):
+                energy = energy + pressed[:, 128 * k : 128 * (k + 1)]
+            r.tile[3:4, :] = energy
+            for k in range(1, wide):
+                copy_of("across", r.tile, r.across.at[gx], beside(k, 0)).start()
+            r.across[gx] = r.tile[...]
+
+        r.total[...] = jnp.zeros_like(r.total)
+
+        def pushes(k, carry):
+            scatter_masters(r.total, r.bundle, masters_out, slaves_in, half * k, half)
+
+            @pl.when(jnp.logical_and(ends, k == 0))
+            def _along():
+                receive("across")
+                part = jnp.sum(r.across[...], axis=0)
+                r.middle[...] = part
+                for j in range(1, group):
+                    copy_of("along", r.middle, r.along.at[gy], beside(0, j)).start()
+                r.along[gy] = part
+
+            return carry
+
+        lax.fori_loop(0, 2, pushes, 0)
+        receive("masters", turn)
+        pull_slaves(r.segments, mine, masters_in, r.places, r.pulls, group)
+        scatter_slaves(r.total, r.segments, r.pulls)
+        applied[...] += total_rows(r.total)
+
+        @pl.when(begins)
+        def _scaled():
+            r.vectors[1] = r.applied[0] * r.inverse[...]
+            pack_halo(NEXT_PLAN, r.vectors.at[1], r.halo_out_next)
+            send_halo(NEXT_PLAN, r.halo_out_next, r.halo_in_next, "halo_next")
+
+        return carry
+
+    lax.fori_loop(0, 2, apply, 0)
+    seed, direction, scaled = r.own[0:192, :], r.vectors[0], r.vectors[1]
+    applied, again = r.applied[0], r.applied[1]
     receive("along")
     totals = jnp.sum(jnp.sum(r.along[...], axis=0), axis=1, keepdims=True)
     first, second, third, fourth = (totals[k : k + 1] for k in range(4))
@@ -923,7 +944,8 @@
     adjoint[...] = forward * direction - aside * scaled
     residual[...] = seed - forward * applied + aside * again
     for kind in KINDS:
-        whole[kind].wait_send()
+        for turn in range(2 if kind in ("slaves", "masters") else 1):
+            all_of(kind, turn).wait_send()
 
 
 def finish_kernel(found, left, adjoint, residual):

time: 42.5 us -> 41 us (0.965)
  Pallas kernels: 41.7 us -> 40.2 us
    pallas_call x1, Pallas kernels: 39.9 us -> 38.4 us  [shards(): pl.pallas_call(functools.partial(whole_kernel, extents, tuple(scratch)),...]
where the time goes in v4:
time: 41 us; the launch traced here: 40.8 us
  Pallas kernels  40.2 us (98%)
  between operations  0.64 us (2%)
    pallas_call x1, Pallas kernels, shards(): pl.pallas_call(functools.partial(whole_kernel, extents, tuple(scratch)),...  38.4 us
    pallas_call x1, Pallas kernels, shards(): pl.pallas_call(finish_kernel, out_shape=[field, field], in_specs=[VMEM, V...  1.82 us

profile of v4, /device:TPU:1, one launch (start us, length us, event | category | flops | bytes accessed | tf_op | source)
XLA Modules:
  0.0 40.8 jit_solution(12836910971064961580)
XLA Ops:
  0.6 38.4 %conjugate_gradients.1 = (f32[192,128]{1,0:T(8,128)}, f32[192,128]{1,0:T(8,128)}) custom-call(f32[3,8,8,128]{3,2,1,0:T(8,128)} %refs_0_.1, f32[8,8,128]{2,1,0:T(8,128)} %refs_1_.1, f32[8,8,128]{2,1,0:T(8,128)} %refs_2_.1, s32[1,1024]{1,0:T(1,128)} %bitcast.2, s32[4,1024]{1,0:T(4,128)} %refs_4_.1, f32[4,1024]{1,0:T(4,128)} %refs_5_.1, s32[4,1024]{1,0:T(4,128)} %refs_6_.1, ...), custom_call_target="tpu_custom_call" | custom-call | tf_op jit(solution)/shard_map/conjugate_gradients/pallas_call | solution.py:987
  39.0 1.8 %finish.1 = (f32[3,8,8,128]{3,2,1,0:T(8,128)}, f32[3,8,8,128]{3,2,1,0:T(8,128)}) custom-call(f32[192,128]{1,0:T(8,128)} %get-tuple-element.4.found, f32[192,128]{1,0:T(8,128)} %get-tuple-element.5.left), custom_call_target="tpu_custom_call" | custom-call | tf_op jit(solution)/shard_map/finish/pallas_call | solution.py:1000

commit v5 on v4

--- a/solution.py
+++ b/solution.py
@@ -498,9 +498,9 @@
     theirs[...] = placed[:, 0:4] + placed[:, 8:12]
 
 
-def gather_masters(table, bundle, theirs, group, first, count):
+def gather_masters(table, bundle, theirs, place, first, count):
     def master(k):
-        source = lax.rem(first + k, group)
+        source = place(first + k)
         theirs[source, 0:3, :] = gather_block(table, bundle[source])
 
     each(0, count, master, GATHER_UNROLL)
@@ -703,8 +703,8 @@
 
 
 def whole_kernel(extents, names, *refs):
-    inputs, (adjoint, residual) = refs[: len(INPUTS)], refs[len(INPUTS) : len(INPUTS) + 2]
-    r = Refs(names, refs[len(INPUTS) + 2 :])
+    inputs, results = refs[: len(INPUTS)], refs[len(INPUTS)]
+    r = Refs(names, refs[len(INPUTS) + 1 :])
     wide, group = extents
     gx, gy = lax.axis_index("gx"), lax.axis_index("gy")
     loads = {
@@ -755,15 +755,29 @@
             part = pl.ds(at, rows)
             copy_of(kind, source.at[part], target.at[part], beside(dx, dy)).start()
 
-    def send_block(source, target, kind, k, turn):
-        device = beside(0, k)
-        copy_of(kind, source.at[device[1]], target.at[gy], device, turn).start()
+    side = math.isqrt(group)
+    offsets = [(dy, dx) for dy in range(side) for dx in range(side) if dy or dx]
+    offsets.sort(key=lambda offset: -sum(min(d, side - d) for d in offset))
+
+    def across_square(dy, dx):
+        row, column = lax.rem(gy // side + dy, side), lax.rem(lax.rem(gy, side) + dx, side)
+        return row * side + column
+
+    def send_block(source, target, kind, to, turn):
+        copy_of(kind, source.at[to], target.at[gy], (gx, to), turn).start()
 
     def send_blocks(source, target, kind, turn=0):
-        for k in range(1, group):
-            send_block(source, target, kind, k, turn)
+        for offset in offsets:
+            send_block(source, target, kind, across_square(*offset), turn)
         target[gy] = source[gy]
 
+    def in_turn(n):
+        return across_square(side // 2 + side - n // side, lax.rem(n, side))
+
+    r.wide[...] = jnp.zeros_like(r.wide)
+    r.mass_wide[...] = jnp.zeros_like(r.mass_wide)
+    r.wide_mod[...] = jnp.zeros_like(r.wide_mod)
+    r.masters_out[...] = jnp.zeros_like(r.masters_out)
     loads["modulus"].wait()
     lay_out([r.modulus], 4, r.own, r.swapped)
     pack_halo(MODULUS_PLAN, r.own, r.modulus_out)
@@ -790,15 +804,11 @@
     )
     send_blocks(r.packed, r.bundle, "packed")
 
-    r.wide[...] = jnp.zeros_like(r.wide)
-    r.mass_wide[...] = jnp.zeros_like(r.mass_wide)
-    r.wide_mod[...] = jnp.zeros_like(r.wide_mod)
     for i in range(3):
         widen_own(r.own, i, r.wide, i)
     widen_own(r.own, 3, r.mass_wide, 0)
     for x in range(4):
         r.wide_mod[pl.ds(8 * (x + 2) + 2, 4), :] = r.own[pl.ds(4 * 64 + 4 * x, 4), :]
-    r.masters_out[...] = jnp.zeros_like(r.masters_out)
 
     def store_modulus(array, parity, start, count, stride, value):
         r.wide_mod[rows_of(start, count, stride), :] = value
@@ -837,14 +847,14 @@
 
         def masters(k, carry):
             first = half * k
-            gather_masters(table_of(r.vectors[turn]), r.bundle, masters_out, group, gy + first, half)
-
-            @pl.when(k > 0)
-            def _middle():
-                send_block(masters_out, masters_in, "masters", first, turn)
+            gather_masters(table_of(r.vectors[turn]), r.bundle, masters_out, in_turn, first, half)
+
+            @pl.when(k == 0)
+            def _other():
+                send_block(masters_out, masters_in, "masters", in_turn(first), turn)
 
             for j in range(1, half):
-                send_block(masters_out, masters_in, "masters", first + j, turn)
+                send_block(masters_out, masters_in, "masters", in_turn(first + j), turn)
             return carry
 
         lax.fori_loop(0, 2, masters, 0)
@@ -863,7 +873,6 @@
 
         @pl.when(ends)
         def _next():
-            r.wide[...] = jnp.zeros_like(r.wide)
             for i in range(3):
                 widen_own(r.vectors.at[1], i, r.wide, i)
             receive("halo_next")
@@ -908,8 +917,9 @@
                 receive("across")
                 part = jnp.sum(r.across[...], axis=0)
                 r.middle[...] = part
-                for j in range(1, group):
-                    copy_of("along", r.middle, r.along.at[gy], beside(0, j)).start()
+                for offset in offsets:
+                    device = (gx, across_square(*offset))
+                    copy_of("along", r.middle, r.along.at[gy], device).start()
                 r.along[gy] = part
 
             return carry
@@ -941,16 +951,16 @@
     step_next = later / curved
     forward = step + step_next * grown
     aside = step_next * step
-    adjoint[...] = forward * direction - aside * scaled
-    residual[...] = seed - forward * applied + aside * again
+    results[0:192, :] = forward * direction - aside * scaled
+    results[192:384, :] = seed - forward * applied + aside * again
     for kind in KINDS:
         for turn in range(2 if kind in ("slaves", "masters") else 1):
             all_of(kind, turn).wait_send()
 
 
-def finish_kernel(found, left, adjoint, residual):
-    for source, ref in ((found, adjoint), (left, residual)):
-        value = reorder(source[...], False)
+def finish_kernel(results, adjoint, residual):
+    values = reorder(results[...], False)
+    for value, ref in ((values[0:192], adjoint), (values[192:384], residual)):
         for i in range(3):
             for x in range(8):
                 for py in range(2):
@@ -983,12 +993,11 @@
         penalty.reshape(1, count),
     )
     scratch = scratch_of(extents, args)
-    own = jax.ShapeDtypeStruct((192, 128), F32)
-    found, left = pl.pallas_call(
+    results = pl.pallas_call(
         functools.partial(whole_kernel, extents, tuple(scratch)),
-        out_shape=[own, own],
+        out_shape=jax.ShapeDtypeStruct((384, 128), F32),
         in_specs=[pl.BlockSpec(memory_space=pl.ANY)] * len(args),
-        out_specs=[VMEM, VMEM],
+        out_specs=VMEM,
         scratch_shapes=list(scratch.values()),
         compiler_params=pltpu.CompilerParams(
             collective_id=1, has_side_effects=True, vmem_limit_bytes=LIMIT
@@ -1000,11 +1009,11 @@
         pl.pallas_call(
             finish_kernel,
             out_shape=[field, field],
-            in_specs=[VMEM, VMEM],
+            in_specs=[VMEM],
             out_specs=[VMEM, VMEM],
             compiler_params=pltpu.CompilerParams(vmem_limit_bytes=LIMIT),
             name="finish",
-        )(found, left)
+        )(results)
     )
 
 

time: 41 us -> 40.6 us (level)
  no operation moved by 1% of the time
where the time goes in v5:
time: 40.6 us; the launch traced here: 40.5 us
  Pallas kernels  39.8 us (98%)
  between operations  0.64 us (2%)
    pallas_call x1, Pallas kernels, shards(): pl.pallas_call(functools.partial(whole_kernel, extents, tuple(scratch)),...  38 us
    pallas_call x1, Pallas kernels, shards(): pl.pallas_call(finish_kernel, out_shape=[field, field], in_specs=[VMEM],...  1.82 us

profile of v5, /device:TPU:1, one launch (start us, length us, event | category | flops | bytes accessed | tf_op | source)
XLA Modules:
  0.0 40.5 jit_solution(12352462446150913052)
XLA Ops:
  0.6 38.0 %conjugate_gradients.1.results = f32[384,128]{1,0:T(8,128)} custom-call(f32[3,8,8,128]{3,2,1,0:T(8,128)} %refs_0_.1, f32[8,8,128]{2,1,0:T(8,128)} %refs_1_.1, f32[8,8,128]{2,1,0:T(8,128)} %refs_2_.1, s32[1,1024]{1,0:T(1,128)} %bitcast.2, s32[4,1024]{1,0:T(4,128)} %refs_4_.1, f32[4,1024]{1,0:T(4,128)} %refs_5_.1, s32[4,1024]{1,0:T(4,128)} %refs_6_.1, ...), custom_call_target="tpu_custom_call" | custom-call | tf_op jit(solution)/shard_map/conjugate_gradients/pallas_call | solution.py:996
  38.7 1.8 %finish.1 = (f32[3,8,8,128]{3,2,1,0:T(8,128)}, f32[3,8,8,128]{3,2,1,0:T(8,128)}) custom-call(f32[384,128]{1,0:T(8,128)} %conjugate_gradients.1.results), custom_call_target="tpu_custom_call" | custom-call | tf_op jit(solution)/shard_map/finish/pallas_call | solution.py:1009

commit v6 on v5

--- a/solution.py
+++ b/solution.py
@@ -885,25 +885,30 @@
             narrow(r.out, i, applied, i)
         mass = r.own[192:256, :]
         applied[...] += jnp.concatenate([mass, mass, mass], axis=0) * r.vectors[turn]
-        receive("slaves", turn)
 
         @pl.when(ends)
-        def _sums():
+        def _early():
             scaled = r.vectors[1]
             r.tile[0:1, :] = inner(r.own[0:192, :], r.vectors[0])
             r.tile[1:2, :] = inner(r.vectors[0], r.applied[0])
             r.tile[2:3, :] = inner(scaled, r.applied[0])
             r.tile[4:8, :] = jnp.zeros((4, 128), F32)
+            r.tile[3:4, :] = inner(scaled, r.applied[1])
+
+        receive("slaves", turn)
+
+        @pl.when(ends)
+        def _sums():
             pressed = jnp.zeros((3, CAP), F32)
             for source in range(group):
                 gap = r.masters_out[1, source, 0:3, :] - r.slaves_in[1, source, 0:3, :]
                 pressed = pressed + r.bundle[source, 4:5, :] * gap * gap
             pressed = jnp.sum(pressed, axis=0, keepdims=True)
-            energy = inner(scaled, r.applied[1])
+            energy = r.tile[3:4, :]
             for k in range(CAP // 128):
                 energy = energy + pressed[:, 128 * k : 128 * (k + 1)]
             r.tile[3:4, :] = energy
-            for k in range(1, wide):
+            for k in sorted(range(1, wide), key=lambda k: -min(k, wide - k)):
                 copy_of("across", r.tile, r.across.at[gx], beside(k, 0)).start()
             r.across[gx] = r.tile[...]
 

time: 40.6 us -> 40.5 us (level)
  no operation moved by 1% of the time
where the time goes in v6:
time: 40.5 us; the launch traced here: 40.3 us
  Pallas kernels  39.7 us (98%)
  between operations  0.64 us (2%)
    pallas_call x1, Pallas kernels, shards(): pl.pallas_call(functools.partial(whole_kernel, extents, tuple(scratch)),...  37.9 us
    pallas_call x1, Pallas kernels, shards(): pl.pallas_call(finish_kernel, out_shape=[field, field], in_specs=[VMEM],...  1.82 us

profile of v6, /device:TPU:1, one launch (start us, length us, event | category | flops | bytes accessed | tf_op | source)
XLA Modules:
  0.0 40.3 jit_solution(9934612858741343803)
XLA Ops:
  0.6 37.9 %conjugate_gradients.1.results = f32[384,128]{1,0:T(8,128)} custom-call(f32[3,8,8,128]{3,2,1,0:T(8,128)} %refs_0_.1, f32[8,8,128]{2,1,0:T(8,128)} %refs_1_.1, f32[8,8,128]{2,1,0:T(8,128)} %refs_2_.1, s32[1,1024]{1,0:T(1,128)} %bitcast.2, s32[4,1024]{1,0:T(4,128)} %refs_4_.1, f32[4,1024]{1,0:T(4,128)} %refs_5_.1, s32[4,1024]{1,0:T(4,128)} %refs_6_.1, ...), custom_call_target="tpu_custom_call" | custom-call | tf_op jit(solution)/shard_map/conjugate_gradients/pallas_call | solution.py:1001
  38.5 1.8 %finish.1 = (f32[3,8,8,128]{3,2,1,0:T(8,128)}, f32[3,8,8,128]{3,2,1,0:T(8,128)}) custom-call(f32[384,128]{1,0:T(8,128)} %conjugate_gradients.1.results), custom_call_target="tpu_custom_call" | custom-call | tf_op jit(solution)/shard_map/finish/pallas_call | solution.py:1014
